TPU v7x, 128 devices: a whole 4x4x4 slice. The times are simulated.
128 devices in a mesh: blk: 32 (over z_hi, y, x), grp: 4 (over z_lo, core).
Axes of the slice: x: 4, y: 4, z: 4 (z_hi: 2, z_lo: 2; z = z_hi * 2 + z_lo), core: 2. Of those that a mesh axis runs over, the one named last changes fastest.
Arguments:
- image_embed: bfloat16 [28672, 512], P(('blk', 'grp')), may hold values from -1 to 1
- text_embed: bfloat16 [28672, 512], P(('blk', 'grp')), may hold values from -1 to 1
Outputs:
- image_grad: float32 [28672, 512], P(('blk', 'grp'))
- text_grad: float32 [28672, 512], P(('blk', 'grp'))
- mean_loss: float32 [1], replicated
All inputs are finite; a program needn't handle non-finite values.
Results may differ from a plain program's by a relative error of at most 0.0023.
Values may be sent and summed in bfloat16 or wider, within the bound.
No kernel may reach another device: no remote copies, remote signals or barrier semaphores. Data moves between devices by JAX's collectives and lax.ppermute only.
A program may use at most 128 MiB of HBM per device.

v0:
```python
import functools
import itertools
import math

import jax
import jax.numpy as jnp
from jax import lax
from jax.experimental import pallas as pl
from jax.experimental.pallas import tpu as pltpu
from jax.sharding import Mesh, PartitionSpec as P

AXES = ("zh", "y", "x", "zl", "c")
A_BITS = ("zp", "yq", "yp")
B_BITS = ("zq", "xq", "xp")
PAIRS = ((0, 0), (1, 0), (1, 1), (0, 1))
SWAP = [(0, 1), (1, 0)]
LOG2E = math.log2(math.e)
LN2 = math.log(2.0)
SCALE = 100.0 * LOG2E
BLOCK = 256
TAIL = 16
TEXT_BLOCKS = 1
PARTS = 4
VMEM_LIMIT = 56 * 1024 * 1024


def forward_kernel(own_ref, other_ref, text_ref, image_ref, pair_ref, row_ref, col_ref, text_t, image, scores, block_max, row_max, row_sum, col_max, col_sum):
    half = own_ref.shape[0]
    columns = text_ref.shape[0]
    count = 2 * half // BLOCK
    text_t[...] = text_ref[...].T
    image[:half, :] = own_ref[...]
    image[half:, :] = other_ref[...]
    col_max[...] = jnp.full(col_max.shape, -1e30, jnp.float32)
    col_sum[...] = jnp.zeros(col_sum.shape, jnp.float32)

    def multiply(index, slot):
        at = pl.multiple_of(jnp.minimum(index, count - 1) * BLOCK, BLOCK)
        rows = image[pl.ds(at, BLOCK), :]
        for start in range(0, columns, BLOCK):
            cols = slice(start, start + BLOCK)
            part = SCALE * jnp.dot(rows, text_t[:, cols], preferred_element_type=jnp.float32)
            scores[slot][:, cols] = part
            block_max[slot][:, cols] = jnp.max(part.reshape(BLOCK // 8, 8, BLOCK), axis=0)

    def sums(index, slot):
        old = col_max[...]
        peak = jnp.maximum(old, block_max[slot][...])
        col_max[...] = peak
        total = col_sum[...] * jnp.exp2(old - peak)
        for start in range(0, BLOCK, 8):
            block = scores[slot][start : start + 8, :]
            pieces = [block[:, k : k + 128] for k in range(0, columns, 128)]
            top = functools.reduce(jnp.maximum, pieces)
            at = pl.multiple_of(index * BLOCK + start, 8)
            row_max[pl.ds(at, 8), :] = top
            row_sum[pl.ds(at, 8), :] = functools.reduce(jnp.add, [jnp.exp2(piece - top) for piece in pieces])
            total = total + jnp.exp2(block - peak)
        col_sum[...] = total

    multiply(0, 0)

    @pl.loop(0, count // 2)
    def _(turn):
        multiply(2 * turn + 1, 1)
        sums(2 * turn, 0)
        multiply(2 * turn + 2, 0)
        sums(2 * turn + 1, 1)

    tops = row_max[...].T
    parts = row_sum[...].T
    peak = jnp.max(tops, axis=0, keepdims=True)
    total = jnp.sum(parts * jnp.exp2(tops - peak), axis=0, keepdims=True)
    row_lse = peak + jnp.log2(total)
    for k in range(2 * half // 128):
        row_ref[k : k + 1, :] = row_lse[:, k * 128 : k * 128 + 128]
    peak = jnp.max(col_max[...], axis=0, keepdims=True)
    total = jnp.sum(col_sum[...] * jnp.exp2(col_max[...] - peak), axis=0, keepdims=True)
    col_lse = peak + jnp.log2(total)
    products = image_ref[...].astype(jnp.float32) * pair_ref[...].astype(jnp.float32)
    diagonal = 100.0 * jnp.sum(jnp.sum(products, axis=0, keepdims=True), axis=1, keepdims=True)
    count = columns // 128
    for place in range(col_ref.shape[0]):
        for k in range(count):
            col_ref[place, k : k + 1, :] = col_lse[:, k * 128 : k * 128 + 128]
        col_ref[place, count:, :] = jnp.broadcast_to(diagonal, (col_ref.shape[1] - count, 128))


def forward(own, other, text, image, pair, members):
    half, width = own.shape
    columns = text.shape[0]
    elements = 2 * half * columns
    f32 = lambda *shape: pltpu.VMEM(shape, jnp.float32)
    return pl.pallas_call(
        forward_kernel,
        out_shape=[
            jax.ShapeDtypeStruct((2 * half // 128, 128), jnp.float32),
            jax.ShapeDtypeStruct((members, columns // 128 + 2, 128), jnp.float32),
        ],
        scratch_shapes=[
            pltpu.VMEM((width, columns), jnp.bfloat16),
            pltpu.VMEM((2 * half, width), jnp.bfloat16),
            [f32(BLOCK, columns), f32(BLOCK, columns)],
            [f32(8, columns), f32(8, columns)],
            f32(2 * half, 128),
            f32(2 * half, 128),
            f32(8, columns),
            f32(8, columns),
        ],
        compiler_params=pltpu.CompilerParams(vmem_limit_bytes=VMEM_LIMIT),
        cost_estimate=pl.CostEstimate(
            flops=2 * elements * width, bytes_accessed=4 * (half + columns) * width, transcendentals=2 * elements
        ),
    )(own, other, text, image, pair)


def tail_of(scalar, width):
    spread = jnp.broadcast_to(scalar, (TAIL, width))
    high = spread.astype(jnp.bfloat16).astype(jnp.float32)
    middle = (spread - high).astype(jnp.bfloat16).astype(jnp.float32)
    low = spread - high - middle
    lane = lax.broadcasted_iota(jnp.int32, (TAIL, width), 1)
    values = jnp.where(lane == 0, high, jnp.where(lane == 1, middle, jnp.where(lane == 2, low, 0.0)))
    return values.astype(jnp.bfloat16)


def whole_lse(parts_ref, lse_ref):
    count = lse_ref.shape[1] // 128
    parts = parts_ref[:, :count, :]
    peak = jnp.max(parts, axis=0)
    value = peak + jnp.log2(jnp.sum(jnp.exp2(parts - peak[None]), axis=0)) + 1.0
    for k in range(count):
        lse_ref[:, k * 128 : k * 128 + 128] = jnp.broadcast_to(value[k : k + 1, :], (8, 128))


def gradient_kernel(unit, pack, *refs):
    if pack:
        index_ref, row_parts, col_parts, rows_ref, first_ref, second_ref, *refs = refs
        out_ref, own_ref, row_ref, col_ref, term_ref, *refs = refs
        whole_lse(row_parts, row_ref)
        whole_lse(col_parts, col_ref)
        lse_sum = jnp.sum(row_ref[0:1, :] - 1.0, axis=1, keepdims=True)
        diagonal = jnp.sum(row_parts[:, row_parts.shape[1] - 1, 0:1], axis=0, keepdims=True)
        term_ref[...] = jnp.broadcast_to(LN2 * lse_sum - 2.0 * diagonal, term_ref.shape)
        column_refs = (first_ref, second_ref)
    else:
        index_ref, row_ref, col_ref, own_rows, other_rows, column_ref, *refs = refs
        mine_ref, out_ref, *refs = refs
        other_refs, (rows_ref, *refs) = refs[:PARTS], refs[PARTS:]
        rows_ref[: other_rows.shape[0], :] = other_rows[...]
        rows_ref[other_rows.shape[0] :, :] = own_rows[...]
        column_refs = (column_ref,)
    columns_t, columns, scores, weights, row_lse, tail = refs
    total = rows_ref.shape[0]
    block = weights[0].shape[0]
    count = total // block
    size = column_refs[0].shape[0]
    for piece, column_ref in enumerate(column_refs):
        part = slice(piece * size, (piece + 1) * size)
        columns_t[:, part] = column_ref[...].T
        columns[part, :] = column_ref[...]
    across = columns.shape[0]
    if pack:
        row_lse[...] = jnp.broadcast_to(row_ref[0:1, :], (128, total)).T
        halves = [col_ref[0:1, : across // 2], col_ref[0:1, across // 2 :]]
        sums = [jnp.sum(half - 1.0, axis=1, keepdims=True) for half in halves]
        tail[...] = tail_of(LN2 * (sums[0] + sums[1]), tail.shape[1])
    else:
        row_lse[: total // 2, :] = jnp.broadcast_to(row_ref[0:1, total // 2 :], (128, total // 2)).T
        row_lse[total // 2 :, :] = jnp.broadcast_to(row_ref[0:1, : total // 2], (128, total // 2)).T

    def rows_at(index):
        if isinstance(index, int):
            return slice(index * block, (index + 1) * block)
        return pl.ds(pl.multiple_of(index * block, block), block)

    def multiply(index, slot):
        rows = rows_ref[rows_at(index), :]
        for start in range(0, across, BLOCK):
            cols = slice(start, start + BLOCK)
            scores[slot][:, cols] = jnp.dot(rows, columns_t[:, cols], preferred_element_type=jnp.float32)

    def weigh(index, slot):
        row_part = row_lse[rows_at(index), :]
        for start in range(0, across, 128):
            cols = slice(start, start + 128)
            scaled = SCALE * scores[slot][:, cols]
            value = jnp.exp2(scaled - row_part) + jnp.exp2(scaled - col_ref[0:1, cols])
            weights[slot][:, cols] = value.astype(jnp.bfloat16)

    def collect(index, slot):
        value = jnp.dot(weights[slot][...], columns[...], preferred_element_type=jnp.float32)
        if not pack:
            if index < PARTS:
                other_refs[index][...] = value.astype(out_ref.dtype)
                return
            out_ref[(index - PARTS) * block : (index - PARTS + 1) * block, :] = value.astype(out_ref.dtype)
            for part in range(block // unit):
                mine = (index - PARTS) * (block // unit) + part == index_ref[0]
                mine_ref[...] = jnp.where(mine, value[part * unit : (part + 1) * unit, :], mine_ref[...])
            return
        for part in range(block // unit):
            place = index * (block // unit) + part
            mine = place == index_ref[0]
            at = pl.multiple_of(place * (unit + TAIL), TAIL)
            piece = value[part * unit : (part + 1) * unit, :]
            out_ref[pl.ds(at, unit), :] = jnp.where(mine, 0.0, piece).astype(out_ref.dtype)
            out_ref[pl.ds(pl.multiple_of(at + unit, TAIL), TAIL), :] = tail[...]
            own_ref[...] = jnp.where(mine, piece, own_ref[...])

    multiply(0, 0)
    multiply(1, 1)
    weigh(0, 0)

    def turns(turn):
        multiply(2 * turn + 2, 0)
        collect(2 * turn, 0)
        weigh(2 * turn + 1, 1)
        multiply(2 * turn + 3, 1)
        collect(2 * turn + 1, 1)
        weigh(2 * turn + 2, 0)

    if pack:
        pl.loop(0, count // 2 - 1)(turns)
    else:
        for turn in range(count // 2 - 1):
            turns(turn)
    collect(count - 2, 0)
    weigh(count - 1, 1)
    collect(count - 1, 1)


def gradient_scratch(total, across, width, block):
    return [
        pltpu.VMEM((width, across), jnp.bfloat16),
        pltpu.VMEM((across, width), jnp.bfloat16),
        [pltpu.VMEM((block, across), jnp.float32)] * 2,
        [pltpu.VMEM((block, across), jnp.bfloat16)] * 2,
        pltpu.VMEM((total, 128), jnp.float32),
        pltpu.VMEM((TAIL, width), jnp.bfloat16),
    ]


def text_gradient(text, own, other, col_parts, row_parts, unit, index):
    total, width = text.shape
    across = 2 * own.shape[0]
    vmem = pl.BlockSpec(memory_space=pltpu.VMEM)
    return pl.pallas_call(
        functools.partial(gradient_kernel, unit, True),
        in_specs=[pl.BlockSpec(memory_space=pltpu.SMEM)] + [vmem] * 5,
        out_shape=[
            jax.ShapeDtypeStruct((total // unit * (unit + TAIL), width), jnp.bfloat16),
            jax.ShapeDtypeStruct((unit, width), jnp.float32),
            jax.ShapeDtypeStruct((8, total), jnp.float32),
            jax.ShapeDtypeStruct((8, across), jnp.float32),
            jax.ShapeDtypeStruct((8, 128), jnp.float32),
        ],
        scratch_shapes=gradient_scratch(total, across, width, TEXT_BLOCKS * unit),
        compiler_params=pltpu.CompilerParams(vmem_limit_bytes=VMEM_LIMIT),
        cost_estimate=pl.CostEstimate(
            flops=4 * total * across * width, bytes_accessed=4 * (total + across) * width, transcendentals=0
        ),
    )(index, col_parts, row_parts, text, own, other)


def image_gradient(own, other, text, row_lse, col_lse, unit, index):
    half, width = own.shape
    across = text.shape[0]
    block = half // PARTS
    return pl.pallas_call(
        functools.partial(gradient_kernel, unit, False),
        in_specs=[pl.BlockSpec(memory_space=pltpu.SMEM)] + [pl.BlockSpec(memory_space=pltpu.VMEM)] * 5,
        out_shape=[
            jax.ShapeDtypeStruct((unit, width), jnp.float32),
            jax.ShapeDtypeStruct((half, width), jnp.bfloat16),
        ]
        + [jax.ShapeDtypeStruct((block, width), jnp.bfloat16)] * PARTS,
        scratch_shapes=[pltpu.VMEM((2 * half, width), jnp.bfloat16)] + gradient_scratch(2 * half, across, width, block),
        compiler_params=pltpu.CompilerParams(vmem_limit_bytes=VMEM_LIMIT),
        cost_estimate=pl.CostEstimate(
            flops=0, bytes_accessed=0, transcendentals=0
        ),
    )(index, row_lse, col_lse, own, other, text)


def pack_kernel(index_ref, term_ref, term_back_ref, part_ref, own_ref, *refs):
    *back_refs, out_ref, mine_ref = refs
    unit = mine_ref.shape[0]
    size = back_refs[0].shape[0]
    tail = tail_of(term_ref[0:1, 0:1] + term_back_ref[0:1, 0:1], out_ref.shape[1])
    for place in range(own_ref.shape[0] // unit):
        part = slice(place * unit, (place + 1) * unit)
        mine = index_ref[0] == place
        start = place * unit % size
        back = back_refs[place * unit // size][start : start + unit, :]
        back = back.astype(jnp.float32)
        value = own_ref[part, :].astype(jnp.float32) + back
        at = place * (unit + TAIL)
        out_ref[at : at + unit, :] = jnp.where(mine, 0.0, value).astype(out_ref.dtype)
        out_ref[at + unit : at + unit + TAIL, :] = tail

        @pl.when(mine)
        def _():
            mine_ref[...] = part_ref[...] + back


def packed(part, own, back, unit, index, terms):
    total, width = own.shape
    smem = pl.BlockSpec(memory_space=pltpu.SMEM)
    vmem = pl.BlockSpec(memory_space=pltpu.VMEM)
    return pl.pallas_call(
        pack_kernel,
        in_specs=[smem] + [vmem] * (4 + len(back)),
        out_shape=[
            jax.ShapeDtypeStruct((total // unit * (unit + TAIL), width), jnp.bfloat16),
            jax.ShapeDtypeStruct((unit, width), jnp.float32),
        ],
        compiler_params=pltpu.CompilerParams(vmem_limit_bytes=VMEM_LIMIT),
        cost_estimate=pl.CostEstimate(flops=0, bytes_accessed=0, transcendentals=0),
    )(index, *terms, part, own, *back)


def finish_kernel(divisor, parts_ref, own_ref, pair_ref, *refs):
    if divisor is None:
        grad_ref, scalar_ref = refs
    else:
        other_ref, grad_ref, loss_ref = refs
    count = parts_ref.shape[0]
    rows = own_ref.shape[0]
    value = own_ref[...] - pair_ref[...].astype(jnp.float32)
    tail = jnp.zeros((TAIL, own_ref.shape[1]), jnp.float32)
    for part in range(count):
        value = value + parts_ref[part, :rows, :].astype(jnp.float32)
        tail = tail + parts_ref[part, rows:, :].astype(jnp.float32)
    grad_ref[...] = 100.0 * value
    if divisor is None:
        scalar_ref[...] = tail
    else:
        loss_ref[0] = jnp.sum(tail[0:1, :] + other_ref[0:1, :]) / divisor


def finished(parts, own, pair, scalars=None, divisor=None):
    vmem = pl.BlockSpec(memory_space=pltpu.VMEM)
    if divisor is None:
        last, place, given = jax.ShapeDtypeStruct((TAIL, own.shape[1]), jnp.float32), vmem, []
    else:
        last, place, given = jax.ShapeDtypeStruct((1,), jnp.float32), pl.BlockSpec(memory_space=pltpu.SMEM), [scalars]
    return pl.pallas_call(
        functools.partial(finish_kernel, divisor),
        in_specs=[vmem] * (3 + len(given)),
        out_specs=[vmem, place],
        out_shape=[jax.ShapeDtypeStruct(own.shape, jnp.float32), last],
        compiler_params=pltpu.CompilerParams(vmem_limit_bytes=VMEM_LIMIT),
    )(parts, own, pair, *given)


def bits_of(x, y, z):
    return {axis + kind: PAIRS[at][k] for axis, at in zip("xyz", (x, y, z)) for k, kind in enumerate("pq")}


def groups_of(names):
    found = {}
    for z, y, x, core in itertools.product(range(4), range(4), range(4), range(2)):
        bits = bits_of(x, y, z)
        key = tuple(bits[name] for name in sorted(bits) if name not in names) + (core,)
        place = functools.reduce(lambda total, name: 2 * total + bits[name], names, 0)
        found.setdefault(key, {})[place] = ((((z // 2) * 4 + y) * 4 + x) * 2 + z % 2) * 2 + core
    return [[group[place] for place in sorted(group)] for group in found.values()]


def own_bits():
    where = {"x": lax.axis_index("x"), "y": lax.axis_index("y"), "z": 2 * lax.axis_index("zh") + lax.axis_index("zl")}
    bits = {}
    for axis, at in where.items():
        bits[axis + "p"] = jnp.where((at == 1) | (at == 2), 1, 0)
        bits[axis + "q"] = at // 2
    return bits


def place_of(names, bits):
    return functools.reduce(lambda total, name: 2 * total + bits[name], names, 0)


def doubled(value, names, name, bits):
    mask = 1 << (len(names) - 1 - names.index(name))
    pairs = [(group[at], group[at ^ mask]) for group in groups_of(names) for at in range(len(group))]
    back = lax.ppermute(value, AXES, pairs)
    at = lax.broadcasted_iota(jnp.int32, (2,) + (1,) * value.ndim, 0)
    return jnp.where(at == bits[name], value[None], back[None])


def gathered(image, text, bits):
    half = image.shape[0] // 2
    pieces = [image[:half], image[half:], text[:half], text[half:]]
    names = [A_BITS, A_BITS, B_BITS, B_BITS]
    for turn in range(3):
        pieces = [
            doubled(piece, name, name[2 - turn] if k % 2 == 0 else name[2 - (2, 0, 1)[turn]], bits)
            for k, (piece, name) in enumerate(zip(pieces, names))
        ]
    whole = []
    for k in (0, 2):
        both = jnp.stack([pieces[k], jnp.transpose(pieces[k + 1], (2, 0, 1, 3, 4))], axis=3)
        whole.append(both.reshape(16 * half, image.shape[1]))
    return lax.optimization_barrier(tuple(whole))


def swap(value):
    return lax.ppermute(value, "c", [(0, 1), (1, 0)])


def exchanged(blocks, names):
    return lax.all_to_all(
        blocks, AXES, split_axis=0, concat_axis=0, tiled=True, axis_index_groups=groups_of(names)
    )


def joined(first, second):
    peak = jnp.maximum(first, second)
    return peak + jnp.log2(jnp.exp2(first - peak) + jnp.exp2(second - peak))


def body(image_embed, text_embed):
    rows, width = image_embed.shape
    bits = own_bits()
    members = 2 ** len(A_BITS)
    half = members * rows
    batch = rows * 2 * members * members
    at_a = jnp.full((1,), place_of(A_BITS, bits), jnp.int32)
    at_b = jnp.full((1,), place_of(B_BITS, bits), jnp.int32)

    own, text = gathered(image_embed, text_embed, bits)
    other = swap(own)
    row_part, col_parts = forward(own, other, text, image_embed, text_embed, members)

    col_parts = exchanged(col_parts, B_BITS)
    count = half // 128
    back = swap(row_part)
    row_part = joined(row_part, jnp.concatenate([back[count:], back[:count]], axis=0))
    row_parts = exchanged(jnp.broadcast_to(row_part[None], (members,) + row_part.shape), A_BITS)

    text_sum, text_own, col_lse, row_lse, term = text_gradient(text, own, other, col_parts, row_parts, rows, at_b)
    term_back = swap(term)
    text_sum, own, other = lax.optimization_barrier((text_sum, own, other))
    text_parts = exchanged(text_sum.reshape(members, rows + TAIL, width), B_BITS)
    image_mine, image_half, *image_other = image_gradient(own, other, text, row_lse, col_lse, rows, at_a)
    image_back = [swap(piece) for piece in image_other]
    image_sum, image_own = packed(image_mine, image_half, image_back, rows, at_a, (term, term_back))
    image_parts = exchanged(image_sum.reshape(members, rows + TAIL, width), A_BITS)
    text_grad, tail_b = finished(text_parts, text_own, image_embed)
    image_grad, mean_loss = finished(image_parts, image_own, text_embed, tail_b, 2.0 * batch)
    return (image_grad, text_grad, mean_loss)


def solution(mesh):
    fine = Mesh(mesh.devices.reshape(2, 4, 4, 2, 2), AXES)
    spec = P(AXES, None)
    return jax.shard_map(body, mesh=fine, in_specs=(spec, spec), out_specs=(spec, spec, P()), check_vma=False)
```

profile of v0, /device:TPU:2, one launch (start us, length us, event | category | flops | bytes accessed | tf_op | source)
XLA Modules:
  0.0 169.6 jit_solution(14299727341009200182)
XLA Ops:
  1.6 4.1 %collective-permute-start.9 = (bf16[112,512]{1,0:T(8,128)(2,1)S(1)}, bf16[112,512]{1,0:T(8,128)(2,1)S(1)}, u32[]{:S(2)}, u32[]{:S(2)}) collective-permute-start(bf16[112,512]{1,0:T(8,128)(2,1)S(1)} %get-tuple-element.52), channel_id=1, source_target_pairs={{0,66},{4,70},{12,78},{8,74},{66,0},{70,4},{78,12},{74,8},{1,67},{... | collective-permute-start | bytes 344072 | tf_op jit(solution)/shard_map/ppermute | solution.py:387
  7.2 1.7 collective-permute-start
  9.1 1.6 collective-permute-start.10
  10.8 1.6 collective-permute-start.7
  12.4 2.9 %collective-permute-start.1 = (bf16[2,112,512]{2,1,0:T(8,128)(2,1)S(1)}, bf16[2,112,512]{2,1,0:T(8,128)(2,1)S(1)}, u32[]{:S(2)}, u32[]{:S(2)}) collective-permute-start(bf16[2,112,512]{2,1,0:T(8,128)(2,1)S(1)} %broadcast_select_fusion.13), channel_id=1, source_target_pairs={{0,48},{16,32},{48,0},{32,16},{2,50},{18,34},{50,2},{34,18},{1,49}... | collective-permute-start | bytes 688136 | tf_op jit(solution)/shard_map/ppermute | solution.py:387
  15.9 2.1 %collective-permute-start.11 = (bf16[2,2,112,512]{3,2,0,1:T(8,128)(2,1)S(1)}, bf16[2,2,112,512]{3,2,0,1:T(8,128)(2,1)S(1)}, u32[]{:S(2)}, u32[]{:S(2)}) collective-permute-start(bf16[2,2,112,512]{3,2,0,1:T(8,128)(2,1)S(1)} %broadcast_select_fusion.4), channel_id=1, source_target_pairs={{0,12},{4,8},{12,0},{8,4},{66,78},{70,74},{78,66},{74,70},{1,13},{... | collective-permute-start | bytes 1376264 | tf_op jit(solution)/shard_map/ppermute | solution.py:387
  18.1 2.2 %collective-permute-start.8 = (bf16[2,2,112,512]{3,2,1,0:T(8,128)(2,1)S(1)}, bf16[2,2,112,512]{3,2,1,0:T(8,128)(2,1)S(1)}, u32[]{:S(2)}, u32[]{:S(2)}) collective-permute-start(bf16[2,2,112,512]{3,2,1,0:T(8,128)(2,1)S(1)} %broadcast_select_fusion.6), channel_id=1, source_target_pairs={{0,66},{4,70},{12,78},{8,74},{66,0},{70,4},{78,12},{74,8},{1,67},{... | collective-permute-start | bytes 1376264 | tf_op jit(solution)/shard_map/ppermute | solution.py:387
  22.1 2.3 %collective-permute-start.5 = (bf16[2,2,112,512]{3,2,0,1:T(8,128)(2,1)S(1)}, bf16[2,2,112,512]{3,2,0,1:T(8,128)(2,1)S(1)}, u32[]{:S(2)}, u32[]{:S(2)}) collective-permute-start(bf16[2,2,112,512]{3,2,0,1:T(8,128)(2,1)S(1)} %broadcast_select_fusion.7), channel_id=1, source_target_pairs={{0,48},{16,32},{48,0},{32,16},{2,50},{18,34},{50,2},{34,18},{1,49}... | collective-permute-start | bytes 1376264 | tf_op jit(solution)/shard_map/ppermute | solution.py:387
  24.6 2.3 %collective-permute-done.11 = bf16[2,2,112,512]{3,2,0,1:T(8,128)(2,1)S(1)} collective-permute-done((bf16[2,2,112,512]{3,2,0,1:T(8,128)(2,1)S(1)}, bf16[2,2,112,512]{3,2,0,1:T(8,128)(2,1)S(1)}, u32[]{:S(2)}, u32[]{:S(2)}) %collective-permute-start.11) | collective-permute-done | bytes 458784 | tf_op jit(solution)/shard_map/ppermute | solution.py:387
  27.1 2.6 %collective-permute-done.8 = bf16[2,2,112,512]{3,2,1,0:T(8,128)(2,1)S(1)} collective-permute-done((bf16[2,2,112,512]{3,2,1,0:T(8,128)(2,1)S(1)}, bf16[2,2,112,512]{3,2,1,0:T(8,128)(2,1)S(1)}, u32[]{:S(2)}, u32[]{:S(2)}) %collective-permute-start.8) | collective-permute-done | bytes 458784 | tf_op jit(solution)/shard_map/ppermute | solution.py:387
  33.3 3.8 %collective-permute-done.12.other_ref.refs_5_.refs_4_ = bf16[1792,512]{1,0:T(8,128)(2,1)S(1)} collective-permute-done((bf16[1792,512]{1,0:T(8,128)(2,1)S(1)}, bf16[1792,512]{1,0:T(8,128)(2,1)S(1)}, u32[]{:S(2)}, u32[]{:S(2)}) %collective-permute-start.12) | collective-permute-done | bytes 1835040 | tf_op jit(solution)/shard_map/ppermute | solution.py:409
  38.3 18.8 %shard_map.49 = (f32[28,128]{1,0:T(8,128)}, f32[8,16,128]{2,1,0:T(8,128)}) custom-call(bf16[1792,512]{1,0:T(8,128)(2,1)} %bitcast.12, bf16[1792,512]{1,0:T(8,128)(2,1)} %copy-done.2, bf16[1792,512]{1,0:T(8,128)(2,1)} %bitcast.8, bf16[224,512]{1,0:T(8,128)(2,1)} %pair_ref.4, bf16[224,512]{1,0:T(8,128)(2,1)} %pair_ref.5), custom_call_target="tpu_custom_call" | custom-call | flops 6576668672 | bytes 7340032 | tf_op jit(solution)/shard_map/pallas_call | solution.py:94
  57.3 5.9 %all-to-all-start = ((f32[8,16,128]{2,1,0:T(8,128)}), f32[8,16,128]{2,1,0:T(8,128)S(1)}, u32[]{:S(2)}, u32[]{:S(2)}) async-start(f32[8,16,128]{2,1,0:T(8,128)} %get-tuple-element.29), calls=%async_computation | async-start | bytes 131072 | tf_op jit(solution)/shard_map/all_to_all | solution.py:413
  64.0 5.3 %all-to-all-done.refs_1_ = f32[8,16,128]{2,1,0:T(8,128)S(1)} async-done(((f32[8,16,128]{2,1,0:T(8,128)}), f32[8,16,128]{2,1,0:T(8,128)S(1)}, u32[]{:S(2)}, u32[]{:S(2)}) %all-to-all-start) | async-done | bytes 65568 | tf_op jit(solution)/shard_map/all_to_all | solution.py:413
  70.0 3.6 %all-to-all-start.1 = ((f32[8,28,128]{2,1,0:T(8,128)}), f32[8,28,128]{2,1,0:T(8,128)S(1)}, u32[]{:S(2)}, u32[]{:S(2)}) async-start(f32[8,28,128]{2,1,0:T(8,128)} %broadcast_in_dim.305), calls=%async_computation.1 | async-start | bytes 262144 | tf_op jit(solution)/shard_map/all_to_all | solution.py:413
  73.6 6.8 %all-to-all-done.1.refs_2_ = f32[8,28,128]{2,1,0:T(8,128)S(1)} async-done(((f32[8,28,128]{2,1,0:T(8,128)}), f32[8,28,128]{2,1,0:T(8,128)S(1)}, u32[]{:S(2)}, u32[]{:S(2)}) %all-to-all-start.1) | async-done | bytes 114720 | tf_op jit(solution)/shard_map/all_to_all | solution.py:413
  81.0 19.6 %shard_map.50 = (bf16[1920,512]{1,0:T(8,128)(2,1)}, f32[224,512]{1,0:T(8,128)}, f32[8,1792]{1,0:T(8,128)}, f32[8,3584]{1,0:T(8,128)}, f32[8,128]{1,0:T(8,128)}) custom-call(s32[1]{0:T(128)} %bitcast.1.refs_0_, f32[8,16,128]{2,1,0:T(8,128)} %copy-done.8, f32[8,28,128]{2,1,0:T(8,128)} %copy-done.7, bf16[1792,512]{1,0:T(8,128)(2,1)} %bitcast.9, ...), custom_call_target="tpu_custom_call" | custom-call | flops 13153337344 | bytes 11010048 | tf_op jit(solution)/shard_map/pallas_call | solution.py:248
  100.7 5.1 %all-to-all-start.3 = ((bf16[8,240,512]{2,1,0:T(8,128)(2,1)}), bf16[8,240,512]{2,1,0:T(8,128)(2,1)S(1)}, u32[]{:S(2)}, u32[]{:S(2)}) async-start(bf16[8,240,512]{2,1,0:T(8,128)(2,1)} %bitcast.15), calls=%async_computation.3 | async-start | bytes 3932160 | tf_op jit(solution)/shard_map/all_to_all | solution.py:413
  105.8 18.6 %shard_map.51 = (f32[224,512]{1,0:T(8,128)}, bf16[1792,512]{1,0:T(8,128)(2,1)}, bf16[448,512]{1,0:T(8,128)(2,1)}, bf16[448,512]{1,0:T(8,128)(2,1)}, bf16[448,512]{1,0:T(8,128)(2,1)}, /*index=5*/bf16[448,512]{1,0:T(8,128)(2,1)}) custom-call(s32[1]{0:T(128)} %bitcast.refs_0_.index_ref, f32[8,3584]{1,0:T(8,128)} %get-tuple-element.32.refs_1_, ...), custom_call_target="tpu_custom_call" | custom-call | tf_op jit(solution)/shard_map/pallas_call | solution.py:270
  129.3 4.3 %shard_map.52 = (bf16[1920,512]{1,0:T(8,128)(2,1)}, f32[224,512]{1,0:T(8,128)}) custom-call(s32[1]{0:T(128)} %bitcast.refs_0_.index_ref, f32[8,128]{1,0:T(8,128)} %get-tuple-element.31.term_ref, f32[8,128]{1,0:T(8,128)} %copy-done.10, f32[224,512]{1,0:T(8,128)} %get-tuple-element.37.part_ref, bf16[1792,512]{1,0:T(8,128)(2,1)} %get-tuple-element.38.own_ref, ...), custom_call_target="tpu_custom_call" | custom-call | tf_op jit(solution)/shard_map/pallas_call | solution.py:311
  134.9 4.3 %all-to-all-start.2 = ((bf16[8,240,512]{2,1,0:T(8,128)(2,1)}), bf16[8,240,512]{2,1,0:T(8,128)(2,1)}, u32[]{:S(2)}, u32[]{:S(2)}) async-start(bf16[8,240,512]{2,1,0:T(8,128)(2,1)} %bitcast.16), calls=%async_computation.2 | async-start | bytes 3932160 | tf_op jit(solution)/shard_map/all_to_all | solution.py:413
  139.3 2.8 %shard_map.53 = (f32[224,512]{1,0:T(8,128)}, f32[16,512]{1,0:T(8,128)}) custom-call(bf16[8,240,512]{2,1,0:T(8,128)(2,1)} %copy-done, f32[224,512]{1,0:T(8,128)} %get-tuple-element.46.own_ref, bf16[224,512]{1,0:T(8,128)(2,1)} %pair_ref.4), custom_call_target="tpu_custom_call" | custom-call | tf_op jit(solution)/shard_map/pallas_call | solution.py:348
  142.1 24.4 %all-to-all-done.2.parts_ref = bf16[8,240,512]{2,1,0:T(8,128)(2,1)} async-done(((bf16[8,240,512]{2,1,0:T(8,128)(2,1)}), bf16[8,240,512]{2,1,0:T(8,128)(2,1)}, u32[]{:S(2)}, u32[]{:S(2)}) %all-to-all-start.2) | async-done | bytes 1966112 | tf_op jit(solution)/shard_map/all_to_all | solution.py:413
  166.4 2.9 %shard_map.54 = (f32[224,512]{1,0:T(8,128)}, f32[1]{0:T(128)}) custom-call(bf16[8,240,512]{2,1,0:T(8,128)(2,1)} %all-to-all-done.2.parts_ref, f32[224,512]{1,0:T(8,128)} %get-tuple-element.44.own_ref, bf16[224,512]{1,0:T(8,128)(2,1)} %pair_ref.5, f32[16,512]{1,0:T(8,128)} %get-tuple-element.47.refs_0_), custom_call_target="tpu_custom_call" | custom-call | tf_op jit(solution)/shard_map/pallas_call | solution.py:348
  (77 shorter events, 18.8 us)
Async XLA Ops:
  1.6 7.4 %collective-permute-start.9 = (bf16[112,512]{1,0:T(8,128)(2,1)S(1)}, bf16[112,512]{1,0:T(8,128)(2,1)S(1)}, u32[]{:S(2)}, u32[]{:S(2)}) collective-permute-start(bf16[112,512]{1,0:T(8,128)(2,1)S(1)} %get-tuple-element.52), channel_id=1, source_target_pairs={{0,66},{4,70},{12,78},{8,74},{66,0},{70,4},{78,12},{74,8},{1,67},{... | collective-permute-start | bytes 344072 | tf_op jit(solution)/shard_map/ppermute | solution.py:387
  5.7 5.0 %collective-permute-start.6 = (bf16[112,512]{1,0:T(8,128)(2,1)S(1)}, bf16[112,512]{1,0:T(8,128)(2,1)S(1)}, u32[]{:S(2)}, u32[]{:S(2)}) collective-permute-start(bf16[112,512]{1,0:T(8,128)(2,1)S(1)} %get-tuple-element.51), channel_id=1, source_target_pairs={{0,4},{4,0},{12,8},{8,12},{66,70},{70,66},{78,74},{74,78},{1,5},{5... | collective-permute-start | bytes 344072 | tf_op jit(solution)/shard_map/ppermute | solution.py:387
  7.2 5.1 %collective-permute-start = (bf16[112,512]{1,0:T(8,128)(2,1)S(1)}, bf16[112,512]{1,0:T(8,128)(2,1)S(1)}, u32[]{:S(2)}, u32[]{:S(2)}) collective-permute-start(bf16[112,512]{1,0:T(8,128)(2,1)S(1)} %get-tuple-element.53), channel_id=1, source_target_pairs={{0,16},{16,0},{48,32},{32,48},{2,18},{18,2},{50,34},{34,50},{1,17}... | collective-permute-start | bytes 344072 | tf_op jit(solution)/shard_map/ppermute | solution.py:387
  8.9 6.5 %collective-permute-start.3 = (bf16[112,512]{1,0:T(8,128)(2,1)S(1)}, bf16[112,512]{1,0:T(8,128)(2,1)S(1)}, u32[]{:S(2)}, u32[]{:S(2)}) collective-permute-start(bf16[112,512]{1,0:T(8,128)(2,1)S(1)} %get-tuple-element.54), channel_id=1, source_target_pairs={{0,2},{16,18},{48,50},{32,34},{2,0},{18,16},{50,48},{34,32},{1,3},... | collective-permute-start | bytes 344072 | tf_op jit(solution)/shard_map/ppermute | solution.py:387
  9.1 6.7 %collective-permute-start.10 = (bf16[2,112,512]{2,1,0:T(8,128)(2,1)S(1)}, bf16[2,112,512]{2,1,0:T(8,128)(2,1)S(1)}, u32[]{:S(2)}, u32[]{:S(2)}) collective-permute-start(bf16[2,112,512]{2,1,0:T(8,128)(2,1)S(1)} %broadcast_select_fusion.10), channel_id=1, source_target_pairs={{0,4},{4,0},{12,8},{8,12},{66,70},{70,66},{78,74},{74,78},{1,5},{5... | collective-permute-start | bytes 688136 | tf_op jit(solution)/shard_map/ppermute | solution.py:387
  10.8 7.3 %collective-permute-start.7 = (bf16[2,112,512]{2,1,0:T(8,128)(2,1)S(1)}, bf16[2,112,512]{2,1,0:T(8,128)(2,1)S(1)}, u32[]{:S(2)}, u32[]{:S(2)}) collective-permute-start(bf16[2,112,512]{2,1,0:T(8,128)(2,1)S(1)} %broadcast_select_fusion.11), channel_id=1, source_target_pairs={{0,12},{4,8},{12,0},{8,4},{66,78},{70,74},{78,66},{74,70},{1,13},{... | collective-permute-start | bytes 688136 | tf_op jit(solution)/shard_map/ppermute | solution.py:387
  12.4 7.9 %collective-permute-start.1 = (bf16[2,112,512]{2,1,0:T(8,128)(2,1)S(1)}, bf16[2,112,512]{2,1,0:T(8,128)(2,1)S(1)}, u32[]{:S(2)}, u32[]{:S(2)}) collective-permute-start(bf16[2,112,512]{2,1,0:T(8,128)(2,1)S(1)} %broadcast_select_fusion.13), channel_id=1, source_target_pairs={{0,48},{16,32},{48,0},{32,16},{2,50},{18,34},{50,2},{34,18},{1,49}... | collective-permute-start | bytes 688136 | tf_op jit(solution)/shard_map/ppermute | solution.py:387
  15.5 6.5 %collective-permute-start.4 = (bf16[2,112,512]{2,1,0:T(8,128)(2,1)S(1)}, bf16[2,112,512]{2,1,0:T(8,128)(2,1)S(1)}, u32[]{:S(2)}, u32[]{:S(2)}) collective-permute-start(bf16[2,112,512]{2,1,0:T(8,128)(2,1)S(1)} %broadcast_select_fusion.12), channel_id=1, source_target_pairs={{0,16},{16,0},{48,32},{32,48},{2,18},{18,2},{50,34},{34,50},{1,17}... | collective-permute-start | bytes 688136 | tf_op jit(solution)/shard_map/ppermute | solution.py:387
  15.9 11.0 %collective-permute-start.11 = (bf16[2,2,112,512]{3,2,0,1:T(8,128)(2,1)S(1)}, bf16[2,2,112,512]{3,2,0,1:T(8,128)(2,1)S(1)}, u32[]{:S(2)}, u32[]{:S(2)}) collective-permute-start(bf16[2,2,112,512]{3,2,0,1:T(8,128)(2,1)S(1)} %broadcast_select_fusion.4), channel_id=1, source_target_pairs={{0,12},{4,8},{12,0},{8,4},{66,78},{70,74},{78,66},{74,70},{1,13},{... | collective-permute-start | bytes 1376264 | tf_op jit(solution)/shard_map/ppermute | solution.py:387
  18.1 11.5 %collective-permute-start.8 = (bf16[2,2,112,512]{3,2,1,0:T(8,128)(2,1)S(1)}, bf16[2,2,112,512]{3,2,1,0:T(8,128)(2,1)S(1)}, u32[]{:S(2)}, u32[]{:S(2)}) collective-permute-start(bf16[2,2,112,512]{3,2,1,0:T(8,128)(2,1)S(1)} %broadcast_select_fusion.6), channel_id=1, source_target_pairs={{0,66},{4,70},{12,78},{8,74},{66,0},{70,4},{78,12},{74,8},{1,67},{... | collective-permute-start | bytes 1376264 | tf_op jit(solution)/shard_map/ppermute | solution.py:387
  20.5 12.4 %collective-permute-start.2 = (bf16[2,2,112,512]{3,2,1,0:T(8,128)(2,1)S(1)}, bf16[2,2,112,512]{3,2,1,0:T(8,128)(2,1)S(1)}, u32[]{:S(2)}, u32[]{:S(2)}) collective-permute-start(bf16[2,2,112,512]{3,2,1,0:T(8,128)(2,1)S(1)} %broadcast_select_fusion.9), channel_id=1, source_target_pairs={{0,2},{16,18},{48,50},{32,34},{2,0},{18,16},{50,48},{34,32},{1,3},... | collective-permute-start | bytes 1376264 | tf_op jit(solution)/shard_map/ppermute | solution.py:387
  22.1 10.6 %collective-permute-start.5 = (bf16[2,2,112,512]{3,2,0,1:T(8,128)(2,1)S(1)}, bf16[2,2,112,512]{3,2,0,1:T(8,128)(2,1)S(1)}, u32[]{:S(2)}, u32[]{:S(2)}) collective-permute-start(bf16[2,2,112,512]{3,2,0,1:T(8,128)(2,1)S(1)} %broadcast_select_fusion.7), channel_id=1, source_target_pairs={{0,48},{16,32},{48,0},{32,16},{2,50},{18,34},{50,2},{34,18},{1,49}... | collective-permute-start | bytes 1376264 | tf_op jit(solution)/shard_map/ppermute | solution.py:387
  33.2 3.9 %collective-permute-start.12 = (bf16[1792,512]{1,0:T(8,128)(2,1)S(1)}, bf16[1792,512]{1,0:T(8,128)(2,1)S(1)}, u32[]{:S(2)}, u32[]{:S(2)}) collective-permute-start(bf16[1792,512]{1,0:T(8,128)(2,1)S(1)} %bitcast.11), channel_id=1, source_target_pairs={{0,1},{1,0},{2,3},{3,2},{4,5},{5,4},{6,7},{7,6},{8,9},{9,8},{10,11... | collective-permute-start | bytes 5505032 | tf_op jit(solution)/shard_map/ppermute | solution.py:409
  57.2 6.1 %collective-permute-start.13 = (f32[28,128]{1,0:T(8,128)}, f32[28,128]{1,0:T(8,128)S(1)}, u32[]{:S(2)}, u32[]{:S(2)}) collective-permute-start(f32[28,128]{1,0:T(8,128)} %get-tuple-element.30), channel_id=1, source_target_pairs={{0,1},{1,0},{2,3},{3,2},{4,5},{5,4},{6,7},{7,6},{8,9},{9,8},{10,11... | collective-permute-start | bytes 43016 | tf_op jit(solution)/shard_map/ppermute | solution.py:409
  57.3 12.0 %all-to-all-start = ((f32[8,16,128]{2,1,0:T(8,128)}), f32[8,16,128]{2,1,0:T(8,128)S(1)}, u32[]{:S(2)}, u32[]{:S(2)}) async-start(f32[8,16,128]{2,1,0:T(8,128)} %get-tuple-element.29), calls=%async_computation | async-start | bytes 131072 | tf_op jit(solution)/shard_map/all_to_all | solution.py:413
  70.0 10.4 %all-to-all-start.1 = ((f32[8,28,128]{2,1,0:T(8,128)}), f32[8,28,128]{2,1,0:T(8,128)S(1)}, u32[]{:S(2)}, u32[]{:S(2)}) async-start(f32[8,28,128]{2,1,0:T(8,128)} %broadcast_in_dim.305), calls=%async_computation.1 | async-start | bytes 262144 | tf_op jit(solution)/shard_map/all_to_all | solution.py:413
  100.7 32.9 %all-to-all-start.3 = ((bf16[8,240,512]{2,1,0:T(8,128)(2,1)}), bf16[8,240,512]{2,1,0:T(8,128)(2,1)S(1)}, u32[]{:S(2)}, u32[]{:S(2)}) async-start(bf16[8,240,512]{2,1,0:T(8,128)(2,1)} %bitcast.15), calls=%async_computation.3 | async-start | bytes 3932160 | tf_op jit(solution)/shard_map/all_to_all | solution.py:413
  105.8 19.7 %copy-start.9 = (f32[8,128]{1,0:T(8,128)S(1)}, f32[8,128]{1,0:T(8,128)}, u32[]{:S(2)}) copy-start(f32[8,128]{1,0:T(8,128)} %get-tuple-element.31.term_ref) | copy-start | bytes 12292
  124.5 2.5 %collective-permute-start.15 = (bf16[448,512]{1,0:T(8,128)(2,1)}, bf16[448,512]{1,0:T(8,128)(2,1)S(1)}, u32[]{:S(2)}, u32[]{:S(2)}) collective-permute-start(bf16[448,512]{1,0:T(8,128)(2,1)} %get-tuple-element.39), channel_id=1, source_target_pairs={{0,1},{1,0},{2,3},{3,2},{4,5},{5,4},{6,7},{7,6},{8,9},{9,8},{10,11... | collective-permute-start | bytes 1376264 | tf_op jit(solution)/shard_map/ppermute | solution.py:409
  124.5 2.7 %collective-permute-start.16 = (bf16[448,512]{1,0:T(8,128)(2,1)}, bf16[448,512]{1,0:T(8,128)(2,1)S(1)}, u32[]{:S(2)}, u32[]{:S(2)}) collective-permute-start(bf16[448,512]{1,0:T(8,128)(2,1)} %get-tuple-element.40), channel_id=1, source_target_pairs={{0,1},{1,0},{2,3},{3,2},{4,5},{5,4},{6,7},{7,6},{8,9},{9,8},{10,11... | collective-permute-start | bytes 1376264 | tf_op jit(solution)/shard_map/ppermute | solution.py:409
  125.0 2.8 %collective-permute-start.17 = (bf16[448,512]{1,0:T(8,128)(2,1)}, bf16[448,512]{1,0:T(8,128)(2,1)S(1)}, u32[]{:S(2)}, u32[]{:S(2)}) collective-permute-start(bf16[448,512]{1,0:T(8,128)(2,1)} %get-tuple-element.41), channel_id=1, source_target_pairs={{0,1},{1,0},{2,3},{3,2},{4,5},{5,4},{6,7},{7,6},{8,9},{9,8},{10,11... | collective-permute-start | bytes 1376264 | tf_op jit(solution)/shard_map/ppermute | solution.py:409
  125.1 3.4 %collective-permute-start.18 = (bf16[448,512]{1,0:T(8,128)(2,1)}, bf16[448,512]{1,0:T(8,128)(2,1)S(1)}, u32[]{:S(2)}, u32[]{:S(2)}) collective-permute-start(bf16[448,512]{1,0:T(8,128)(2,1)} %get-tuple-element.42), channel_id=1, source_target_pairs={{0,1},{1,0},{2,3},{3,2},{4,5},{5,4},{6,7},{7,6},{8,9},{9,8},{10,11... | collective-permute-start | bytes 1376264 | tf_op jit(solution)/shard_map/ppermute | solution.py:409
  125.5 1.5 collective-permute-start.14
  134.9 31.5 %all-to-all-start.2 = ((bf16[8,240,512]{2,1,0:T(8,128)(2,1)}), bf16[8,240,512]{2,1,0:T(8,128)(2,1)}, u32[]{:S(2)}, u32[]{:S(2)}) async-start(bf16[8,240,512]{2,1,0:T(8,128)(2,1)} %bitcast.16), calls=%async_computation.2 | async-start | bytes 3932160 | tf_op jit(solution)/shard_map/all_to_all | solution.py:413
  (10 other events, 24.2 us)
where the time goes:
time: 170 us
  Pallas kernels  67.1 us (39%)
  waiting for transfers between devices  49.7 us (29%)
  starting transfers between devices  40.9 us (24%)
  local copies, waits for them, and re-layouts  6.73 us (4%)
  other arithmetic  4.06 us (2%)
    all_to_all x4, waiting for transfers between devices, exchanged(): lax.all_to_all(blocks, AXES, split_axis=0, concat_axis=0, tiled=True, axi...  36.5 us
    ppermute x12, starting transfers between devices, doubled(): back = lax.ppermute(value, AXES, pairs)  20.6 us
    pallas_call x1, Pallas kernels, text_gradient(): pl.pallas_call(functools.partial(gradient_kernel, unit, True), in_specs=[...  19.6 us
    all_to_all x4, starting transfers between devices, exchanged(): lax.all_to_all(blocks, AXES, split_axis=0, concat_axis=0, tiled=True, axi...  19 us
    pallas_call x1, Pallas kernels, forward(): pl.pallas_call(forward_kernel, out_shape=[jax.ShapeDtypeStruct((2 * half...  18.8 us
    pallas_call x1, Pallas kernels, image_gradient(): pl.pallas_call(functools.partial(gradient_kernel, unit, False), in_specs=...  18.6 us
    ppermute x7, waiting for transfers between devices, swap(): return lax.ppermute(value, 'c', [(0, 1), (1, 0)])  6.66 us
    ppermute x12, waiting for transfers between devices, doubled(): back = lax.ppermute(value, AXES, pairs)  6.52 us
  transfers between devices with their start and end apart: 23, of which 12 were waited for; matrix products, arithmetic and copies ran while one was open for 3% of the time, Pallas kernels for 15%

commit v1 on v0

--- a/solution.py
+++ b/solution.py
@@ -382,9 +382,7 @@
 
 
 def doubled(value, names, name, bits):
-    mask = 1 << (len(names) - 1 - names.index(name))
-    pairs = [(group[at], group[at ^ mask]) for group in groups_of(names) for at in range(len(group))]
-    back = lax.ppermute(value, AXES, pairs)
+    back = partner(value, names, name)
     at = lax.broadcasted_iota(jnp.int32, (2,) + (1,) * value.ndim, 0)
     return jnp.where(at == bits[name], value[None], back[None])
 
@@ -405,6 +403,12 @@
     return lax.optimization_barrier(tuple(whole))
 
 
+def partner(value, names, name):
+    mask = 1 << (len(names) - 1 - names.index(name))
+    pairs = [(group[at], group[at ^ mask]) for group in groups_of(names) for at in range(len(group))]
+    return lax.ppermute(value, AXES, pairs)
+
+
 def swap(value):
     return lax.ppermute(value, "c", [(0, 1), (1, 0)])
 
@@ -431,10 +435,13 @@
 
     own, text = gathered(image_embed, text_embed, bits)
     other = swap(own)
-    row_part, col_parts = forward(own, other, text, image_embed, text_embed, members)
-
-    col_parts = exchanged(col_parts, B_BITS)
+    row_part, col_parts = forward(own, other, text, image_embed, text_embed, 1)
+
     count = half // 128
+    kind = lax.broadcasted_iota(jnp.int32, col_parts.shape, 1)
+    for name in B_BITS:
+        back = partner(col_parts, B_BITS, name)
+        col_parts = jnp.where(kind < count, joined(col_parts, back), col_parts + back)
     back = swap(row_part)
     row_part = joined(row_part, jnp.concatenate([back[count:], back[:count]], axis=0))
     row_parts = exchanged(jnp.broadcast_to(row_part[None], (members,) + row_part.shape), A_BITS)

time: 170 us -> 172 us (1.012)
  starting transfers between devices: 40.9 us -> 42.7 us
    ppermute x12 -> x15, starting transfers between devices: 20.6 us -> 28 us  [partner(): return lax.ppermute(value, AXES, pairs)]
    all_to_all x4 -> x3, waiting for transfers between devices: 36.5 us -> 30.5 us  [exchanged(): lax.all_to_all(blocks, AXES, split_axis=0, concat_axis=0, tiled=True, axi...]
    all_to_all x4 -> x3, starting transfers between devices: 19 us -> 13.5 us  [exchanged(): lax.all_to_all(blocks, AXES, split_axis=0, concat_axis=0, tiled=True, axi...]
    ppermute x12 -> x15, waiting for transfers between devices: 6.52 us -> 10.9 us  [partner(): return lax.ppermute(value, AXES, pairs)]
    unnamed x22 -> x20, local copies, waits for them, and re-layouts: 4.11 us -> 4.11 us
  transfers between devices with their start and end apart: 23 -> 25, of which waited for: 12 -> 13; matrix products, arithmetic and copies ran while one was open for 3% -> 4% of each run, Pallas kernels for 15% -> 15%
where the time goes in v1:
time: 172 us; the launch traced here: 171 us
  Pallas kernels  67 us (39%)
  waiting for transfers between devices  48 us (28%)
  starting transfers between devices  42.7 us (25%)
  local copies, waits for them, and re-layouts  6.72 us (4%)
  other arithmetic  5.58 us (3%)
    all_to_all x3, waiting for transfers between devices, exchanged(): lax.all_to_all(blocks, AXES, split_axis=0, concat_axis=0, tiled=True, axi...  30.5 us
    ppermute x15, starting transfers between devices, partner(): return lax.ppermute(value, AXES, pairs)  28 us
    pallas_call x1, Pallas kernels, text_gradient(): pl.pallas_call(functools.partial(gradient_kernel, unit, True), in_specs=[...  19.6 us
    pallas_call x1, Pallas kernels, forward(): pl.pallas_call(forward_kernel, out_shape=[jax.ShapeDtypeStruct((2 * half...  18.7 us
    pallas_call x1, Pallas kernels, image_gradient(): pl.pallas_call(functools.partial(gradient_kernel, unit, False), in_specs=...  18.6 us
    all_to_all x3, starting transfers between devices, exchanged(): lax.all_to_all(blocks, AXES, split_axis=0, concat_axis=0, tiled=True, axi...  13.5 us
    ppermute x15, waiting for transfers between devices, partner(): return lax.ppermute(value, AXES, pairs)  10.9 us
    ppermute x7, waiting for transfers between devices, swap(): return lax.ppermute(value, 'c', [(0, 1), (1, 0)])  6.66 us
  transfers between devices with their start and end apart: 25, of which 13 were waited for; matrix products, arithmetic and copies ran while one was open for 4% of the time, Pallas kernels for 15%

profile of v1, /device:TPU:2, one launch (start us, length us, event | category | flops | bytes accessed | tf_op | source)
XLA Modules:
  0.0 171.1 jit_solution(2684421906219182652)
XLA Ops:
  1.6 4.1 %collective-permute-start.9 = (bf16[112,512]{1,0:T(8,128)(2,1)S(1)}, bf16[112,512]{1,0:T(8,128)(2,1)S(1)}, u32[]{:S(2)}, u32[]{:S(2)}) collective-permute-start(bf16[112,512]{1,0:T(8,128)(2,1)S(1)} %get-tuple-element.52), channel_id=1, source_target_pairs={{0,66},{4,70},{12,78},{8,74},{66,0},{70,4},{78,12},{74,8},{1,67},{... | collective-permute-start | bytes 344072 | tf_op jit(solution)/shard_map/ppermute | solution.py:409
  12.4 2.9 %collective-permute-start.1 = (bf16[2,112,512]{2,1,0:T(8,128)(2,1)S(1)}, bf16[2,112,512]{2,1,0:T(8,128)(2,1)S(1)}, u32[]{:S(2)}, u32[]{:S(2)}) collective-permute-start(bf16[2,112,512]{2,1,0:T(8,128)(2,1)S(1)} %broadcast_select_fusion.13), channel_id=1, source_target_pairs={{0,48},{16,32},{48,0},{32,16},{2,50},{18,34},{50,2},{34,18},{1,49}... | collective-permute-start | bytes 688136 | tf_op jit(solution)/shard_map/ppermute | solution.py:409
  15.9 2.1 %collective-permute-start.11 = (bf16[2,2,112,512]{3,2,0,1:T(8,128)(2,1)S(1)}, bf16[2,2,112,512]{3,2,0,1:T(8,128)(2,1)S(1)}, u32[]{:S(2)}, u32[]{:S(2)}) collective-permute-start(bf16[2,2,112,512]{3,2,0,1:T(8,128)(2,1)S(1)} %broadcast_select_fusion.4), channel_id=1, source_target_pairs={{0,12},{4,8},{12,0},{8,4},{66,78},{70,74},{78,66},{74,70},{1,13},{... | collective-permute-start | bytes 1376264 | tf_op jit(solution)/shard_map/ppermute | solution.py:409
  18.2 2.2 %collective-permute-start.8 = (bf16[2,2,112,512]{3,2,1,0:T(8,128)(2,1)S(1)}, bf16[2,2,112,512]{3,2,1,0:T(8,128)(2,1)S(1)}, u32[]{:S(2)}, u32[]{:S(2)}) collective-permute-start(bf16[2,2,112,512]{3,2,1,0:T(8,128)(2,1)S(1)} %broadcast_select_fusion.6), channel_id=1, source_target_pairs={{0,66},{4,70},{12,78},{8,74},{66,0},{70,4},{78,12},{74,8},{1,67},{... | collective-permute-start | bytes 1376264 | tf_op jit(solution)/shard_map/ppermute | solution.py:409
  22.1 2.3 %collective-permute-start.5 = (bf16[2,2,112,512]{3,2,0,1:T(8,128)(2,1)S(1)}, bf16[2,2,112,512]{3,2,0,1:T(8,128)(2,1)S(1)}, u32[]{:S(2)}, u32[]{:S(2)}) collective-permute-start(bf16[2,2,112,512]{3,2,0,1:T(8,128)(2,1)S(1)} %broadcast_select_fusion.7), channel_id=1, source_target_pairs={{0,48},{16,32},{48,0},{32,16},{2,50},{18,34},{50,2},{34,18},{1,49}... | collective-permute-start | bytes 1376264 | tf_op jit(solution)/shard_map/ppermute | solution.py:409
  24.6 2.3 %collective-permute-done.11 = bf16[2,2,112,512]{3,2,0,1:T(8,128)(2,1)S(1)} collective-permute-done((bf16[2,2,112,512]{3,2,0,1:T(8,128)(2,1)S(1)}, bf16[2,2,112,512]{3,2,0,1:T(8,128)(2,1)S(1)}, u32[]{:S(2)}, u32[]{:S(2)}) %collective-permute-start.11) | collective-permute-done | bytes 458784 | tf_op jit(solution)/shard_map/ppermute | solution.py:409
  27.1 2.6 %collective-permute-done.8 = bf16[2,2,112,512]{3,2,1,0:T(8,128)(2,1)S(1)} collective-permute-done((bf16[2,2,112,512]{3,2,1,0:T(8,128)(2,1)S(1)}, bf16[2,2,112,512]{3,2,1,0:T(8,128)(2,1)S(1)}, u32[]{:S(2)}, u32[]{:S(2)}) %collective-permute-start.8) | collective-permute-done | bytes 458784 | tf_op jit(solution)/shard_map/ppermute | solution.py:409
  33.3 3.8 %collective-permute-done.12.other_ref.refs_5_.refs_4_ = bf16[1792,512]{1,0:T(8,128)(2,1)S(1)} collective-permute-done((bf16[1792,512]{1,0:T(8,128)(2,1)S(1)}, bf16[1792,512]{1,0:T(8,128)(2,1)S(1)}, u32[]{:S(2)}, u32[]{:S(2)}) %collective-permute-start.12) | collective-permute-done | bytes 1835040 | tf_op jit(solution)/shard_map/ppermute | solution.py:413
  38.3 18.7 %shard_map.49 = (f32[28,128]{1,0:T(8,128)}, f32[1,16,128]{2,1,0:T(8,128)}) custom-call(bf16[1792,512]{1,0:T(8,128)(2,1)} %bitcast.12, bf16[1792,512]{1,0:T(8,128)(2,1)} %copy-done.2, bf16[1792,512]{1,0:T(8,128)(2,1)} %bitcast.8, bf16[224,512]{1,0:T(8,128)(2,1)} %pair_ref.4, bf16[224,512]{1,0:T(8,128)(2,1)} %pair_ref.5), custom_call_target="tpu_custom_call" | custom-call | flops 6576668672 | bytes 7340032 | tf_op jit(solution)/shard_map/pallas_call | solution.py:94
  57.1 2.6 %collective-permute-start.13 = (f32[1,16,128]{2,1,0:T(8,128)}, f32[1,16,128]{2,1,0:T(8,128)S(1)}, u32[]{:S(2)}, u32[]{:S(2)}) collective-permute-start(f32[1,16,128]{2,1,0:T(8,128)} %get-tuple-element.29), channel_id=1, source_target_pairs={{0,66},{4,70},{12,78},{8,74},{66,0},{70,4},{78,12},{74,8},{1,67},{... | collective-permute-start | bytes 24584 | tf_op jit(solution)/shard_map/ppermute | solution.py:409
  59.7 2.5 %collective-permute-done.13 = f32[1,16,128]{2,1,0:T(8,128)S(1)} collective-permute-done((f32[1,16,128]{2,1,0:T(8,128)}, f32[1,16,128]{2,1,0:T(8,128)S(1)}, u32[]{:S(2)}, u32[]{:S(2)}) %collective-permute-start.13) | collective-permute-done | bytes 8224 | tf_op jit(solution)/shard_map/ppermute | solution.py:409
  62.9 1.8 %collective-permute-start.14 = (f32[1,16,128]{2,1,0:T(8,128)S(1)}, f32[1,16,128]{2,1,0:T(8,128)S(1)}, u32[]{:S(2)}, u32[]{:S(2)}) collective-permute-start(f32[1,16,128]{2,1,0:T(8,128)S(1)} %add_select_fusion.2), channel_id=1, source_target_pairs={{0,12},{4,8},{12,0},{8,4},{66,78},{70,74},{78,66},{74,70},{1,13},{... | collective-permute-start | bytes 24584 | tf_op jit(solution)/shard_map/ppermute | solution.py:409
  64.7 1.9 %collective-permute-done.14 = f32[1,16,128]{2,1,0:T(8,128)S(1)} collective-permute-done((f32[1,16,128]{2,1,0:T(8,128)S(1)}, f32[1,16,128]{2,1,0:T(8,128)S(1)}, u32[]{:S(2)}, u32[]{:S(2)}) %collective-permute-start.14) | collective-permute-done | bytes 8224 | tf_op jit(solution)/shard_map/ppermute | solution.py:409
  66.7 3.0 %collective-permute-start.15 = (f32[1,16,128]{2,1,0:T(8,128)S(1)}, f32[1,16,128]{2,1,0:T(8,128)S(1)}, u32[]{:S(2)}, u32[]{:S(2)}) collective-permute-start(f32[1,16,128]{2,1,0:T(8,128)S(1)} %add_select_fusion.1), channel_id=1, source_target_pairs={{0,4},{4,0},{12,8},{8,12},{66,70},{70,66},{78,74},{74,78},{1,5},{5... | collective-permute-start | bytes 24584 | tf_op jit(solution)/shard_map/ppermute | solution.py:409
  71.1 3.6 %all-to-all-start = ((f32[8,28,128]{2,1,0:T(8,128)}), f32[8,28,128]{2,1,0:T(8,128)S(1)}, u32[]{:S(2)}, u32[]{:S(2)}) async-start(f32[8,28,128]{2,1,0:T(8,128)} %broadcast_in_dim.305), calls=%async_computation | async-start | bytes 262144 | tf_op jit(solution)/shard_map/all_to_all | solution.py:417
  75.3 6.1 %all-to-all-done.refs_2_ = f32[8,28,128]{2,1,0:T(8,128)S(1)} async-done(((f32[8,28,128]{2,1,0:T(8,128)}), f32[8,28,128]{2,1,0:T(8,128)S(1)}, u32[]{:S(2)}, u32[]{:S(2)}) %all-to-all-start) | async-done | bytes 114720 | tf_op jit(solution)/shard_map/all_to_all | solution.py:417
  82.1 19.6 %shard_map.50 = (bf16[1920,512]{1,0:T(8,128)(2,1)}, f32[224,512]{1,0:T(8,128)}, f32[8,1792]{1,0:T(8,128)}, f32[8,3584]{1,0:T(8,128)}, f32[8,128]{1,0:T(8,128)}) custom-call(s32[1]{0:T(128)} %bitcast.1.refs_0_, f32[1,16,128]{2,1,0:T(8,128)} %add_select_fusion.refs_1_, f32[8,28,128]{2,1,0:T(8,128)} %copy-done.7, bf16[1792,512]{1,0:T(8,128)(2,1)} %bitcast.9, ...), custom_call_target="tpu_custom_call" | custom-call | flops 13153337344 | bytes 11010048 | tf_op jit(solution)/shard_map/pallas_call | solution.py:248
  101.8 5.6 %all-to-all-start.2 = ((bf16[8,240,512]{2,1,0:T(8,128)(2,1)}), bf16[8,240,512]{2,1,0:T(8,128)(2,1)S(1)}, u32[]{:S(2)}, u32[]{:S(2)}) async-start(bf16[8,240,512]{2,1,0:T(8,128)(2,1)} %bitcast.15), calls=%async_computation.2 | async-start | bytes 3932160 | tf_op jit(solution)/shard_map/all_to_all | solution.py:417
  107.4 18.6 %shard_map.51 = (f32[224,512]{1,0:T(8,128)}, bf16[1792,512]{1,0:T(8,128)(2,1)}, bf16[448,512]{1,0:T(8,128)(2,1)}, bf16[448,512]{1,0:T(8,128)(2,1)}, bf16[448,512]{1,0:T(8,128)(2,1)}, /*index=5*/bf16[448,512]{1,0:T(8,128)(2,1)}) custom-call(s32[1]{0:T(128)} %bitcast.refs_0_.index_ref, f32[8,3584]{1,0:T(8,128)} %get-tuple-element.32.refs_1_, ...), custom_call_target="tpu_custom_call" | custom-call | tf_op jit(solution)/shard_map/pallas_call | solution.py:270
  130.8 4.3 %shard_map.52 = (bf16[1920,512]{1,0:T(8,128)(2,1)}, f32[224,512]{1,0:T(8,128)}) custom-call(s32[1]{0:T(128)} %bitcast.refs_0_.index_ref, f32[8,128]{1,0:T(8,128)} %get-tuple-element.31.term_ref, f32[8,128]{1,0:T(8,128)} %copy-done.9, f32[224,512]{1,0:T(8,128)} %get-tuple-element.37.part_ref, bf16[1792,512]{1,0:T(8,128)(2,1)} %get-tuple-element.38.own_ref, ...), custom_call_target="tpu_custom_call" | custom-call | tf_op jit(solution)/shard_map/pallas_call | solution.py:311
  136.5 4.3 %all-to-all-start.1 = ((bf16[8,240,512]{2,1,0:T(8,128)(2,1)}), bf16[8,240,512]{2,1,0:T(8,128)(2,1)}, u32[]{:S(2)}, u32[]{:S(2)}) async-start(bf16[8,240,512]{2,1,0:T(8,128)(2,1)} %bitcast.16), calls=%async_computation.1 | async-start | bytes 3932160 | tf_op jit(solution)/shard_map/all_to_all | solution.py:417
  140.8 2.8 %shard_map.53 = (f32[224,512]{1,0:T(8,128)}, f32[16,512]{1,0:T(8,128)}) custom-call(bf16[8,240,512]{2,1,0:T(8,128)(2,1)} %copy-done, f32[224,512]{1,0:T(8,128)} %get-tuple-element.46.own_ref, bf16[224,512]{1,0:T(8,128)(2,1)} %pair_ref.4), custom_call_target="tpu_custom_call" | custom-call | tf_op jit(solution)/shard_map/pallas_call | solution.py:348
  143.6 24.4 %all-to-all-done.1.parts_ref = bf16[8,240,512]{2,1,0:T(8,128)(2,1)} async-done(((bf16[8,240,512]{2,1,0:T(8,128)(2,1)}), bf16[8,240,512]{2,1,0:T(8,128)(2,1)}, u32[]{:S(2)}, u32[]{:S(2)}) %all-to-all-start.1) | async-done | bytes 1966112 | tf_op jit(solution)/shard_map/all_to_all | solution.py:417
  168.0 2.9 %shard_map.54 = (f32[224,512]{1,0:T(8,128)}, f32[1]{0:T(128)}) custom-call(bf16[8,240,512]{2,1,0:T(8,128)(2,1)} %all-to-all-done.1.parts_ref, f32[224,512]{1,0:T(8,128)} %get-tuple-element.44.own_ref, bf16[224,512]{1,0:T(8,128)(2,1)} %pair_ref.5, f32[16,512]{1,0:T(8,128)} %get-tuple-element.47.refs_0_), custom_call_target="tpu_custom_call" | custom-call | tf_op jit(solution)/shard_map/pallas_call | solution.py:348
  (83 shorter events, 25.0 us)
Async XLA Ops:
  1.6 7.4 %collective-permute-start.9 = (bf16[112,512]{1,0:T(8,128)(2,1)S(1)}, bf16[112,512]{1,0:T(8,128)(2,1)S(1)}, u32[]{:S(2)}, u32[]{:S(2)}) collective-permute-start(bf16[112,512]{1,0:T(8,128)(2,1)S(1)} %get-tuple-element.52), channel_id=1, source_target_pairs={{0,66},{4,70},{12,78},{8,74},{66,0},{70,4},{78,12},{74,8},{1,67},{... | collective-permute-start | bytes 344072 | tf_op jit(solution)/shard_map/ppermute | solution.py:409
  5.7 5.0 %collective-permute-start.6 = (bf16[112,512]{1,0:T(8,128)(2,1)S(1)}, bf16[112,512]{1,0:T(8,128)(2,1)S(1)}, u32[]{:S(2)}, u32[]{:S(2)}) collective-permute-start(bf16[112,512]{1,0:T(8,128)(2,1)S(1)} %get-tuple-element.51), channel_id=1, source_target_pairs={{0,4},{4,0},{12,8},{8,12},{66,70},{70,66},{78,74},{74,78},{1,5},{5... | collective-permute-start | bytes 344072 | tf_op jit(solution)/shard_map/ppermute | solution.py:409
  7.2 5.1 %collective-permute-start = (bf16[112,512]{1,0:T(8,128)(2,1)S(1)}, bf16[112,512]{1,0:T(8,128)(2,1)S(1)}, u32[]{:S(2)}, u32[]{:S(2)}) collective-permute-start(bf16[112,512]{1,0:T(8,128)(2,1)S(1)} %get-tuple-element.53), channel_id=1, source_target_pairs={{0,16},{16,0},{48,32},{32,48},{2,18},{18,2},{50,34},{34,50},{1,17}... | collective-permute-start | bytes 344072 | tf_op jit(solution)/shard_map/ppermute | solution.py:409
  8.9 6.5 %collective-permute-start.3 = (bf16[112,512]{1,0:T(8,128)(2,1)S(1)}, bf16[112,512]{1,0:T(8,128)(2,1)S(1)}, u32[]{:S(2)}, u32[]{:S(2)}) collective-permute-start(bf16[112,512]{1,0:T(8,128)(2,1)S(1)} %get-tuple-element.54), channel_id=1, source_target_pairs={{0,2},{16,18},{48,50},{32,34},{2,0},{18,16},{50,48},{34,32},{1,3},... | collective-permute-start | bytes 344072 | tf_op jit(solution)/shard_map/ppermute | solution.py:409
  9.1 6.7 %collective-permute-start.10 = (bf16[2,112,512]{2,1,0:T(8,128)(2,1)S(1)}, bf16[2,112,512]{2,1,0:T(8,128)(2,1)S(1)}, u32[]{:S(2)}, u32[]{:S(2)}) collective-permute-start(bf16[2,112,512]{2,1,0:T(8,128)(2,1)S(1)} %broadcast_select_fusion.10), channel_id=1, source_target_pairs={{0,4},{4,0},{12,8},{8,12},{66,70},{70,66},{78,74},{74,78},{1,5},{5... | collective-permute-start | bytes 688136 | tf_op jit(solution)/shard_map/ppermute | solution.py:409
  10.8 7.3 %collective-permute-start.7 = (bf16[2,112,512]{2,1,0:T(8,128)(2,1)S(1)}, bf16[2,112,512]{2,1,0:T(8,128)(2,1)S(1)}, u32[]{:S(2)}, u32[]{:S(2)}) collective-permute-start(bf16[2,112,512]{2,1,0:T(8,128)(2,1)S(1)} %broadcast_select_fusion.11), channel_id=1, source_target_pairs={{0,12},{4,8},{12,0},{8,4},{66,78},{70,74},{78,66},{74,70},{1,13},{... | collective-permute-start | bytes 688136 | tf_op jit(solution)/shard_map/ppermute | solution.py:409
  12.4 7.9 %collective-permute-start.1 = (bf16[2,112,512]{2,1,0:T(8,128)(2,1)S(1)}, bf16[2,112,512]{2,1,0:T(8,128)(2,1)S(1)}, u32[]{:S(2)}, u32[]{:S(2)}) collective-permute-start(bf16[2,112,512]{2,1,0:T(8,128)(2,1)S(1)} %broadcast_select_fusion.13), channel_id=1, source_target_pairs={{0,48},{16,32},{48,0},{32,16},{2,50},{18,34},{50,2},{34,18},{1,49}... | collective-permute-start | bytes 688136 | tf_op jit(solution)/shard_map/ppermute | solution.py:409
  15.5 6.5 %collective-permute-start.4 = (bf16[2,112,512]{2,1,0:T(8,128)(2,1)S(1)}, bf16[2,112,512]{2,1,0:T(8,128)(2,1)S(1)}, u32[]{:S(2)}, u32[]{:S(2)}) collective-permute-start(bf16[2,112,512]{2,1,0:T(8,128)(2,1)S(1)} %broadcast_select_fusion.12), channel_id=1, source_target_pairs={{0,16},{16,0},{48,32},{32,48},{2,18},{18,2},{50,34},{34,50},{1,17}... | collective-permute-start | bytes 688136 | tf_op jit(solution)/shard_map/ppermute | solution.py:409
  15.9 11.0 %collective-permute-start.11 = (bf16[2,2,112,512]{3,2,0,1:T(8,128)(2,1)S(1)}, bf16[2,2,112,512]{3,2,0,1:T(8,128)(2,1)S(1)}, u32[]{:S(2)}, u32[]{:S(2)}) collective-permute-start(bf16[2,2,112,512]{3,2,0,1:T(8,128)(2,1)S(1)} %broadcast_select_fusion.4), channel_id=1, source_target_pairs={{0,12},{4,8},{12,0},{8,4},{66,78},{70,74},{78,66},{74,70},{1,13},{... | collective-permute-start | bytes 1376264 | tf_op jit(solution)/shard_map/ppermute | solution.py:409
  18.2 11.5 %collective-permute-start.8 = (bf16[2,2,112,512]{3,2,1,0:T(8,128)(2,1)S(1)}, bf16[2,2,112,512]{3,2,1,0:T(8,128)(2,1)S(1)}, u32[]{:S(2)}, u32[]{:S(2)}) collective-permute-start(bf16[2,2,112,512]{3,2,1,0:T(8,128)(2,1)S(1)} %broadcast_select_fusion.6), channel_id=1, source_target_pairs={{0,66},{4,70},{12,78},{8,74},{66,0},{70,4},{78,12},{74,8},{1,67},{... | collective-permute-start | bytes 1376264 | tf_op jit(solution)/shard_map/ppermute | solution.py:409
  20.5 12.4 %collective-permute-start.2 = (bf16[2,2,112,512]{3,2,1,0:T(8,128)(2,1)S(1)}, bf16[2,2,112,512]{3,2,1,0:T(8,128)(2,1)S(1)}, u32[]{:S(2)}, u32[]{:S(2)}) collective-permute-start(bf16[2,2,112,512]{3,2,1,0:T(8,128)(2,1)S(1)} %broadcast_select_fusion.9), channel_id=1, source_target_pairs={{0,2},{16,18},{48,50},{32,34},{2,0},{18,16},{50,48},{34,32},{1,3},... | collective-permute-start | bytes 1376264 | tf_op jit(solution)/shard_map/ppermute | solution.py:409
  22.1 10.6 %collective-permute-start.5 = (bf16[2,2,112,512]{3,2,0,1:T(8,128)(2,1)S(1)}, bf16[2,2,112,512]{3,2,0,1:T(8,128)(2,1)S(1)}, u32[]{:S(2)}, u32[]{:S(2)}) collective-permute-start(bf16[2,2,112,512]{3,2,0,1:T(8,128)(2,1)S(1)} %broadcast_select_fusion.7), channel_id=1, source_target_pairs={{0,48},{16,32},{48,0},{32,16},{2,50},{18,34},{50,2},{34,18},{1,49}... | collective-permute-start | bytes 1376264 | tf_op jit(solution)/shard_map/ppermute | solution.py:409
  33.2 3.9 %collective-permute-start.12 = (bf16[1792,512]{1,0:T(8,128)(2,1)S(1)}, bf16[1792,512]{1,0:T(8,128)(2,1)S(1)}, u32[]{:S(2)}, u32[]{:S(2)}) collective-permute-start(bf16[1792,512]{1,0:T(8,128)(2,1)S(1)} %bitcast.11), channel_id=1, source_target_pairs={{0,1},{1,0},{2,3},{3,2},{4,5},{5,4},{6,7},{7,6},{8,9},{9,8},{10,11... | collective-permute-start | bytes 5505032 | tf_op jit(solution)/shard_map/ppermute | solution.py:413
  57.1 5.1 %collective-permute-start.13 = (f32[1,16,128]{2,1,0:T(8,128)}, f32[1,16,128]{2,1,0:T(8,128)S(1)}, u32[]{:S(2)}, u32[]{:S(2)}) collective-permute-start(f32[1,16,128]{2,1,0:T(8,128)} %get-tuple-element.29), channel_id=1, source_target_pairs={{0,66},{4,70},{12,78},{8,74},{66,0},{70,4},{78,12},{74,8},{1,67},{... | collective-permute-start | bytes 24584 | tf_op jit(solution)/shard_map/ppermute | solution.py:409
  59.7 5.0 %collective-permute-start.16 = (f32[28,128]{1,0:T(8,128)}, f32[28,128]{1,0:T(8,128)S(1)}, u32[]{:S(2)}, u32[]{:S(2)}) collective-permute-start(f32[28,128]{1,0:T(8,128)} %get-tuple-element.30), channel_id=1, source_target_pairs={{0,1},{1,0},{2,3},{3,2},{4,5},{5,4},{6,7},{7,6},{8,9},{9,8},{10,11... | collective-permute-start | bytes 43016 | tf_op jit(solution)/shard_map/ppermute | solution.py:413
  62.9 3.7 %collective-permute-start.14 = (f32[1,16,128]{2,1,0:T(8,128)S(1)}, f32[1,16,128]{2,1,0:T(8,128)S(1)}, u32[]{:S(2)}, u32[]{:S(2)}) collective-permute-start(f32[1,16,128]{2,1,0:T(8,128)S(1)} %add_select_fusion.2), channel_id=1, source_target_pairs={{0,12},{4,8},{12,0},{8,4},{66,78},{70,74},{78,66},{74,70},{1,13},{... | collective-permute-start | bytes 24584 | tf_op jit(solution)/shard_map/ppermute | solution.py:409
  66.7 8.0 %collective-permute-start.15 = (f32[1,16,128]{2,1,0:T(8,128)S(1)}, f32[1,16,128]{2,1,0:T(8,128)S(1)}, u32[]{:S(2)}, u32[]{:S(2)}) collective-permute-start(f32[1,16,128]{2,1,0:T(8,128)S(1)} %add_select_fusion.1), channel_id=1, source_target_pairs={{0,4},{4,0},{12,8},{8,12},{66,70},{70,66},{78,74},{74,78},{1,5},{5... | collective-permute-start | bytes 24584 | tf_op jit(solution)/shard_map/ppermute | solution.py:409
  71.1 10.4 %all-to-all-start = ((f32[8,28,128]{2,1,0:T(8,128)}), f32[8,28,128]{2,1,0:T(8,128)S(1)}, u32[]{:S(2)}, u32[]{:S(2)}) async-start(f32[8,28,128]{2,1,0:T(8,128)} %broadcast_in_dim.305), calls=%async_computation | async-start | bytes 262144 | tf_op jit(solution)/shard_map/all_to_all | solution.py:417
  101.8 33.3 %all-to-all-start.2 = ((bf16[8,240,512]{2,1,0:T(8,128)(2,1)}), bf16[8,240,512]{2,1,0:T(8,128)(2,1)S(1)}, u32[]{:S(2)}, u32[]{:S(2)}) async-start(bf16[8,240,512]{2,1,0:T(8,128)(2,1)} %bitcast.15), calls=%async_computation.2 | async-start | bytes 3932160 | tf_op jit(solution)/shard_map/all_to_all | solution.py:417
  126.0 2.5 %collective-permute-start.18 = (bf16[448,512]{1,0:T(8,128)(2,1)}, bf16[448,512]{1,0:T(8,128)(2,1)S(1)}, u32[]{:S(2)}, u32[]{:S(2)}) collective-permute-start(bf16[448,512]{1,0:T(8,128)(2,1)} %get-tuple-element.39), channel_id=1, source_target_pairs={{0,1},{1,0},{2,3},{3,2},{4,5},{5,4},{6,7},{7,6},{8,9},{9,8},{10,11... | collective-permute-start | bytes 1376264 | tf_op jit(solution)/shard_map/ppermute | solution.py:413
  126.0 2.7 %collective-permute-start.19 = (bf16[448,512]{1,0:T(8,128)(2,1)}, bf16[448,512]{1,0:T(8,128)(2,1)S(1)}, u32[]{:S(2)}, u32[]{:S(2)}) collective-permute-start(bf16[448,512]{1,0:T(8,128)(2,1)} %get-tuple-element.40), channel_id=1, source_target_pairs={{0,1},{1,0},{2,3},{3,2},{4,5},{5,4},{6,7},{7,6},{8,9},{9,8},{10,11... | collective-permute-start | bytes 1376264 | tf_op jit(solution)/shard_map/ppermute | solution.py:413
  126.5 2.8 %collective-permute-start.20 = (bf16[448,512]{1,0:T(8,128)(2,1)}, bf16[448,512]{1,0:T(8,128)(2,1)S(1)}, u32[]{:S(2)}, u32[]{:S(2)}) collective-permute-start(bf16[448,512]{1,0:T(8,128)(2,1)} %get-tuple-element.41), channel_id=1, source_target_pairs={{0,1},{1,0},{2,3},{3,2},{4,5},{5,4},{6,7},{7,6},{8,9},{9,8},{10,11... | collective-permute-start | bytes 1376264 | tf_op jit(solution)/shard_map/ppermute | solution.py:413
  126.6 3.4 %collective-permute-start.21 = (bf16[448,512]{1,0:T(8,128)(2,1)}, bf16[448,512]{1,0:T(8,128)(2,1)S(1)}, u32[]{:S(2)}, u32[]{:S(2)}) collective-permute-start(bf16[448,512]{1,0:T(8,128)(2,1)} %get-tuple-element.42), channel_id=1, source_target_pairs={{0,1},{1,0},{2,3},{3,2},{4,5},{5,4},{6,7},{7,6},{8,9},{9,8},{10,11... | collective-permute-start | bytes 1376264 | tf_op jit(solution)/shard_map/ppermute | solution.py:413
  136.5 31.5 %all-to-all-start.1 = ((bf16[8,240,512]{2,1,0:T(8,128)(2,1)}), bf16[8,240,512]{2,1,0:T(8,128)(2,1)}, u32[]{:S(2)}, u32[]{:S(2)}) async-start(bf16[8,240,512]{2,1,0:T(8,128)(2,1)} %bitcast.16), calls=%async_computation.1 | async-start | bytes 3932160 | tf_op jit(solution)/shard_map/all_to_all | solution.py:417
  (11 other events, 34.3 us)

commit v2 on v1

--- a/solution.py
+++ b/solution.py
@@ -442,9 +442,11 @@
     for name in B_BITS:
         back = partner(col_parts, B_BITS, name)
         col_parts = jnp.where(kind < count, joined(col_parts, back), col_parts + back)
+    row_parts = exchanged(jnp.broadcast_to(row_part[None], (members,) + row_part.shape), A_BITS)
+    peak = jnp.max(row_parts, axis=0)
+    row_part = peak + jnp.log2(jnp.sum(jnp.exp2(row_parts - peak[None]), axis=0))
     back = swap(row_part)
-    row_part = joined(row_part, jnp.concatenate([back[count:], back[:count]], axis=0))
-    row_parts = exchanged(jnp.broadcast_to(row_part[None], (members,) + row_part.shape), A_BITS)
+    row_parts = joined(row_part, jnp.concatenate([back[count:], back[:count]], axis=0))[None]
 
     text_sum, text_own, col_lse, row_lse, term = text_gradient(text, own, other, col_parts, row_parts, rows, at_b)
     term_back = swap(term)

time: 172 us -> 169 us (0.983)
  waiting for transfers between devices: 48 us -> 45.3 us
    ppermute x15, waiting for transfers between devices: 10.9 us -> 8.94 us  [partner(): return lax.ppermute(value, AXES, pairs)]
    unnamed x20 -> x18, local copies, waits for them, and re-layouts: 4.11 us -> 3.41 us
where the time goes in v2:
time: 169 us; the launch traced here: 168 us
  Pallas kernels  67 us (40%)
  waiting for transfers between devices  45.3 us (27%)
  starting transfers between devices  42.4 us (25%)
  local copies, waits for them, and re-layouts  6.73 us (4%)
  other arithmetic  5.55 us (3%)
    all_to_all x3, waiting for transfers between devices, exchanged(): lax.all_to_all(blocks, AXES, split_axis=0, concat_axis=0, tiled=True, axi...  29.2 us
    ppermute x15, starting transfers between devices, partner(): return lax.ppermute(value, AXES, pairs)  26.9 us
    pallas_call x1, Pallas kernels, text_gradient(): pl.pallas_call(functools.partial(gradient_kernel, unit, True), in_specs=[...  19.6 us
    pallas_call x1, Pallas kernels, forward(): pl.pallas_call(forward_kernel, out_shape=[jax.ShapeDtypeStruct((2 * half...  18.7 us
    pallas_call x1, Pallas kernels, image_gradient(): pl.pallas_call(functools.partial(gradient_kernel, unit, False), in_specs=...  18.6 us
    all_to_all x3, starting transfers between devices, exchanged(): lax.all_to_all(blocks, AXES, split_axis=0, concat_axis=0, tiled=True, axi...  14 us
    ppermute x15, waiting for transfers between devices, partner(): return lax.ppermute(value, AXES, pairs)  8.94 us
    ppermute x7, waiting for transfers between devices, swap(): return lax.ppermute(value, 'c', [(0, 1), (1, 0)])  7.14 us
  transfers between devices with their start and end apart: 25, of which 13 were waited for; matrix products, arithmetic and copies ran while one was open for 4% of the time, Pallas kernels for 15%

profile of v2, /device:TPU:2, one launch (start us, length us, event | category | flops | bytes accessed | tf_op | source)
XLA Modules:
  0.0 168.0 jit_solution(8376318987154045495)
XLA Ops:
  1.6 4.1 %collective-permute-start.9 = (bf16[112,512]{1,0:T(8,128)(2,1)S(1)}, bf16[112,512]{1,0:T(8,128)(2,1)S(1)}, u32[]{:S(2)}, u32[]{:S(2)}) collective-permute-start(bf16[112,512]{1,0:T(8,128)(2,1)S(1)} %get-tuple-element.52), channel_id=1, source_target_pairs={{0,66},{4,70},{12,78},{8,74},{66,0},{70,4},{78,12},{74,8},{1,67},{... | collective-permute-start | bytes 344072 | tf_op jit(solution)/shard_map/ppermute | solution.py:409
  7.2 1.7 collective-permute-start
  12.4 2.9 %collective-permute-start.1 = (bf16[2,112,512]{2,1,0:T(8,128)(2,1)S(1)}, bf16[2,112,512]{2,1,0:T(8,128)(2,1)S(1)}, u32[]{:S(2)}, u32[]{:S(2)}) collective-permute-start(bf16[2,112,512]{2,1,0:T(8,128)(2,1)S(1)} %broadcast_select_fusion.13), channel_id=1, source_target_pairs={{0,48},{16,32},{48,0},{32,16},{2,50},{18,34},{50,2},{34,18},{1,49}... | collective-permute-start | bytes 688136 | tf_op jit(solution)/shard_map/ppermute | solution.py:409
  15.9 2.1 %collective-permute-start.11 = (bf16[2,2,112,512]{3,2,0,1:T(8,128)(2,1)S(1)}, bf16[2,2,112,512]{3,2,0,1:T(8,128)(2,1)S(1)}, u32[]{:S(2)}, u32[]{:S(2)}) collective-permute-start(bf16[2,2,112,512]{3,2,0,1:T(8,128)(2,1)S(1)} %broadcast_select_fusion.4), channel_id=1, source_target_pairs={{0,12},{4,8},{12,0},{8,4},{66,78},{70,74},{78,66},{74,70},{1,13},{... | collective-permute-start | bytes 1376264 | tf_op jit(solution)/shard_map/ppermute | solution.py:409
  18.2 2.2 %collective-permute-start.8 = (bf16[2,2,112,512]{3,2,1,0:T(8,128)(2,1)S(1)}, bf16[2,2,112,512]{3,2,1,0:T(8,128)(2,1)S(1)}, u32[]{:S(2)}, u32[]{:S(2)}) collective-permute-start(bf16[2,2,112,512]{3,2,1,0:T(8,128)(2,1)S(1)} %broadcast_select_fusion.6), channel_id=1, source_target_pairs={{0,66},{4,70},{12,78},{8,74},{66,0},{70,4},{78,12},{74,8},{1,67},{... | collective-permute-start | bytes 1376264 | tf_op jit(solution)/shard_map/ppermute | solution.py:409
  22.1 2.3 %collective-permute-start.5 = (bf16[2,2,112,512]{3,2,0,1:T(8,128)(2,1)S(1)}, bf16[2,2,112,512]{3,2,0,1:T(8,128)(2,1)S(1)}, u32[]{:S(2)}, u32[]{:S(2)}) collective-permute-start(bf16[2,2,112,512]{3,2,0,1:T(8,128)(2,1)S(1)} %broadcast_select_fusion.7), channel_id=1, source_target_pairs={{0,48},{16,32},{48,0},{32,16},{2,50},{18,34},{50,2},{34,18},{1,49}... | collective-permute-start | bytes 1376264 | tf_op jit(solution)/shard_map/ppermute | solution.py:409
  24.6 2.3 %collective-permute-done.11 = bf16[2,2,112,512]{3,2,0,1:T(8,128)(2,1)S(1)} collective-permute-done((bf16[2,2,112,512]{3,2,0,1:T(8,128)(2,1)S(1)}, bf16[2,2,112,512]{3,2,0,1:T(8,128)(2,1)S(1)}, u32[]{:S(2)}, u32[]{:S(2)}) %collective-permute-start.11) | collective-permute-done | bytes 458784 | tf_op jit(solution)/shard_map/ppermute | solution.py:409
  27.1 2.6 %collective-permute-done.8 = bf16[2,2,112,512]{3,2,1,0:T(8,128)(2,1)S(1)} collective-permute-done((bf16[2,2,112,512]{3,2,1,0:T(8,128)(2,1)S(1)}, bf16[2,2,112,512]{3,2,1,0:T(8,128)(2,1)S(1)}, u32[]{:S(2)}, u32[]{:S(2)}) %collective-permute-start.8) | collective-permute-done | bytes 458784 | tf_op jit(solution)/shard_map/ppermute | solution.py:409
  33.3 3.8 %collective-permute-done.12.other_ref.refs_5_.refs_4_ = bf16[1792,512]{1,0:T(8,128)(2,1)S(1)} collective-permute-done((bf16[1792,512]{1,0:T(8,128)(2,1)S(1)}, bf16[1792,512]{1,0:T(8,128)(2,1)S(1)}, u32[]{:S(2)}, u32[]{:S(2)}) %collective-permute-start.12) | collective-permute-done | bytes 1835040 | tf_op jit(solution)/shard_map/ppermute | solution.py:413
  38.3 18.7 %shard_map.49 = (f32[28,128]{1,0:T(8,128)}, f32[1,16,128]{2,1,0:T(8,128)}) custom-call(bf16[1792,512]{1,0:T(8,128)(2,1)} %bitcast.41, bf16[1792,512]{1,0:T(8,128)(2,1)} %copy-done.2, bf16[1792,512]{1,0:T(8,128)(2,1)} %bitcast.37, bf16[224,512]{1,0:T(8,128)(2,1)} %pair_ref.4, bf16[224,512]{1,0:T(8,128)(2,1)} %pair_ref.5), custom_call_target="tpu_custom_call" | custom-call | flops 6576668672 | bytes 7340032 | tf_op jit(solution)/shard_map/pallas_call | solution.py:94
  57.1 2.6 %collective-permute-start.13 = (f32[1,16,128]{2,1,0:T(8,128)}, f32[1,16,128]{2,1,0:T(8,128)S(1)}, u32[]{:S(2)}, u32[]{:S(2)}) collective-permute-start(f32[1,16,128]{2,1,0:T(8,128)} %get-tuple-element.29), channel_id=1, source_target_pairs={{0,66},{4,70},{12,78},{8,74},{66,0},{70,4},{78,12},{74,8},{1,67},{... | collective-permute-start | bytes 24584 | tf_op jit(solution)/shard_map/ppermute | solution.py:409
  59.7 2.5 %collective-permute-done.13 = f32[1,16,128]{2,1,0:T(8,128)S(1)} collective-permute-done((f32[1,16,128]{2,1,0:T(8,128)}, f32[1,16,128]{2,1,0:T(8,128)S(1)}, u32[]{:S(2)}, u32[]{:S(2)}) %collective-permute-start.13) | collective-permute-done | bytes 8224 | tf_op jit(solution)/shard_map/ppermute | solution.py:409
  62.9 1.8 %collective-permute-start.14 = (f32[1,16,128]{2,1,0:T(8,128)S(1)}, f32[1,16,128]{2,1,0:T(8,128)S(1)}, u32[]{:S(2)}, u32[]{:S(2)}) collective-permute-start(f32[1,16,128]{2,1,0:T(8,128)S(1)} %add_select_fusion.2), channel_id=1, source_target_pairs={{0,12},{4,8},{12,0},{8,4},{66,78},{70,74},{78,66},{74,70},{1,13},{... | collective-permute-start | bytes 24584 | tf_op jit(solution)/shard_map/ppermute | solution.py:409
  66.0 3.4 %all-to-all-start = ((f32[8,28,128]{2,1,0:T(8,128)}), f32[8,28,128]{2,1,0:T(8,128)S(1)}, u32[]{:S(2)}, u32[]{:S(2)}) async-start(f32[8,28,128]{2,1,0:T(8,128)} %broadcast_in_dim.307), calls=%async_computation | async-start | bytes 262144 | tf_op jit(solution)/shard_map/all_to_all | solution.py:417
  69.5 1.9 %collective-permute-start.15 = (f32[1,16,128]{2,1,0:T(8,128)S(1)}, f32[1,16,128]{2,1,0:T(8,128)S(1)}, u32[]{:S(2)}, u32[]{:S(2)}) collective-permute-start(f32[1,16,128]{2,1,0:T(8,128)S(1)} %add_select_fusion.1), channel_id=1, source_target_pairs={{0,4},{4,0},{12,8},{8,12},{66,70},{70,66},{78,74},{74,78},{1,5},{5... | collective-permute-start | bytes 24584 | tf_op jit(solution)/shard_map/ppermute | solution.py:409
  71.4 4.8 %all-to-all-done = f32[8,28,128]{2,1,0:T(8,128)S(1)} async-done(((f32[8,28,128]{2,1,0:T(8,128)}), f32[8,28,128]{2,1,0:T(8,128)S(1)}, u32[]{:S(2)}, u32[]{:S(2)}) %all-to-all-start) | async-done | bytes 114720 | tf_op jit(solution)/shard_map/all_to_all | solution.py:417
  78.4 19.6 %shard_map.50 = (bf16[1920,512]{1,0:T(8,128)(2,1)}, f32[224,512]{1,0:T(8,128)}, f32[8,1792]{1,0:T(8,128)}, f32[8,3584]{1,0:T(8,128)}, f32[8,128]{1,0:T(8,128)}) custom-call(s32[1]{0:T(128)} %bitcast.1.refs_0_, f32[1,16,128]{2,1,0:T(8,128)} %add_select_fusion.refs_1_, f32[1,28,128]{2,1,0:T(8,128)} %fusion.5.refs_2_, bf16[1792,512]{1,0:T(8,128)(2,1)} %bitcast.38, ...), custom_call_target="tpu_custom_call" | custom-call | flops 13153337344 | bytes 11010048 | tf_op jit(solution)/shard_map/pallas_call | solution.py:248
  98.0 6.3 %all-to-all-start.2 = ((bf16[8,240,512]{2,1,0:T(8,128)(2,1)}), bf16[8,240,512]{2,1,0:T(8,128)(2,1)S(1)}, u32[]{:S(2)}, u32[]{:S(2)}) async-start(bf16[8,240,512]{2,1,0:T(8,128)(2,1)} %bitcast.44), calls=%async_computation.2 | async-start | bytes 3932160 | tf_op jit(solution)/shard_map/all_to_all | solution.py:417
  104.3 18.6 %shard_map.51 = (f32[224,512]{1,0:T(8,128)}, bf16[1792,512]{1,0:T(8,128)(2,1)}, bf16[448,512]{1,0:T(8,128)(2,1)}, bf16[448,512]{1,0:T(8,128)(2,1)}, bf16[448,512]{1,0:T(8,128)(2,1)}, /*index=5*/bf16[448,512]{1,0:T(8,128)(2,1)}) custom-call(s32[1]{0:T(128)} %bitcast.refs_0_.index_ref, f32[8,3584]{1,0:T(8,128)} %get-tuple-element.32.refs_1_, ...), custom_call_target="tpu_custom_call" | custom-call | tf_op jit(solution)/shard_map/pallas_call | solution.py:270
  127.7 4.3 %shard_map.52 = (bf16[1920,512]{1,0:T(8,128)(2,1)}, f32[224,512]{1,0:T(8,128)}) custom-call(s32[1]{0:T(128)} %bitcast.refs_0_.index_ref, f32[8,128]{1,0:T(8,128)} %get-tuple-element.31.term_ref, f32[8,128]{1,0:T(8,128)} %copy-done.8, f32[224,512]{1,0:T(8,128)} %get-tuple-element.37.part_ref, bf16[1792,512]{1,0:T(8,128)(2,1)} %get-tuple-element.38.own_ref, ...), custom_call_target="tpu_custom_call" | custom-call | tf_op jit(solution)/shard_map/pallas_call | solution.py:311
  133.4 4.3 %all-to-all-start.1 = ((bf16[8,240,512]{2,1,0:T(8,128)(2,1)}), bf16[8,240,512]{2,1,0:T(8,128)(2,1)}, u32[]{:S(2)}, u32[]{:S(2)}) async-start(bf16[8,240,512]{2,1,0:T(8,128)(2,1)} %bitcast.45), calls=%async_computation.1 | async-start | bytes 3932160 | tf_op jit(solution)/shard_map/all_to_all | solution.py:417
  137.7 2.8 %shard_map.53 = (f32[224,512]{1,0:T(8,128)}, f32[16,512]{1,0:T(8,128)}) custom-call(bf16[8,240,512]{2,1,0:T(8,128)(2,1)} %copy-done, f32[224,512]{1,0:T(8,128)} %get-tuple-element.46.own_ref, bf16[224,512]{1,0:T(8,128)(2,1)} %pair_ref.4), custom_call_target="tpu_custom_call" | custom-call | tf_op jit(solution)/shard_map/pallas_call | solution.py:348
  140.5 24.4 %all-to-all-done.1.parts_ref = bf16[8,240,512]{2,1,0:T(8,128)(2,1)} async-done(((bf16[8,240,512]{2,1,0:T(8,128)(2,1)}), bf16[8,240,512]{2,1,0:T(8,128)(2,1)}, u32[]{:S(2)}, u32[]{:S(2)}) %all-to-all-start.1) | async-done | bytes 1966112 | tf_op jit(solution)/shard_map/all_to_all | solution.py:417
  164.8 2.9 %shard_map.54 = (f32[224,512]{1,0:T(8,128)}, f32[1]{0:T(128)}) custom-call(bf16[8,240,512]{2,1,0:T(8,128)(2,1)} %all-to-all-done.1.parts_ref, f32[224,512]{1,0:T(8,128)} %get-tuple-element.44.own_ref, bf16[224,512]{1,0:T(8,128)(2,1)} %pair_ref.5, f32[16,512]{1,0:T(8,128)} %get-tuple-element.47.refs_0_), custom_call_target="tpu_custom_call" | custom-call | tf_op jit(solution)/shard_map/pallas_call | solution.py:348
  (84 shorter events, 24.1 us)
Async XLA Ops:
  1.6 7.4 %collective-permute-start.9 = (bf16[112,512]{1,0:T(8,128)(2,1)S(1)}, bf16[112,512]{1,0:T(8,128)(2,1)S(1)}, u32[]{:S(2)}, u32[]{:S(2)}) collective-permute-start(bf16[112,512]{1,0:T(8,128)(2,1)S(1)} %get-tuple-element.52), channel_id=1, source_target_pairs={{0,66},{4,70},{12,78},{8,74},{66,0},{70,4},{78,12},{74,8},{1,67},{... | collective-permute-start | bytes 344072 | tf_op jit(solution)/shard_map/ppermute | solution.py:409
  5.7 5.0 %collective-permute-start.6 = (bf16[112,512]{1,0:T(8,128)(2,1)S(1)}, bf16[112,512]{1,0:T(8,128)(2,1)S(1)}, u32[]{:S(2)}, u32[]{:S(2)}) collective-permute-start(bf16[112,512]{1,0:T(8,128)(2,1)S(1)} %get-tuple-element.51), channel_id=1, source_target_pairs={{0,4},{4,0},{12,8},{8,12},{66,70},{70,66},{78,74},{74,78},{1,5},{5... | collective-permute-start | bytes 344072 | tf_op jit(solution)/shard_map/ppermute | solution.py:409
  7.2 5.1 %collective-permute-start = (bf16[112,512]{1,0:T(8,128)(2,1)S(1)}, bf16[112,512]{1,0:T(8,128)(2,1)S(1)}, u32[]{:S(2)}, u32[]{:S(2)}) collective-permute-start(bf16[112,512]{1,0:T(8,128)(2,1)S(1)} %get-tuple-element.53), channel_id=1, source_target_pairs={{0,16},{16,0},{48,32},{32,48},{2,18},{18,2},{50,34},{34,50},{1,17}... | collective-permute-start | bytes 344072 | tf_op jit(solution)/shard_map/ppermute | solution.py:409
  8.9 6.5 %collective-permute-start.3 = (bf16[112,512]{1,0:T(8,128)(2,1)S(1)}, bf16[112,512]{1,0:T(8,128)(2,1)S(1)}, u32[]{:S(2)}, u32[]{:S(2)}) collective-permute-start(bf16[112,512]{1,0:T(8,128)(2,1)S(1)} %get-tuple-element.54), channel_id=1, source_target_pairs={{0,2},{16,18},{48,50},{32,34},{2,0},{18,16},{50,48},{34,32},{1,3},... | collective-permute-start | bytes 344072 | tf_op jit(solution)/shard_map/ppermute | solution.py:409
  9.1 6.7 %collective-permute-start.10 = (bf16[2,112,512]{2,1,0:T(8,128)(2,1)S(1)}, bf16[2,112,512]{2,1,0:T(8,128)(2,1)S(1)}, u32[]{:S(2)}, u32[]{:S(2)}) collective-permute-start(bf16[2,112,512]{2,1,0:T(8,128)(2,1)S(1)} %broadcast_select_fusion.10), channel_id=1, source_target_pairs={{0,4},{4,0},{12,8},{8,12},{66,70},{70,66},{78,74},{74,78},{1,5},{5... | collective-permute-start | bytes 688136 | tf_op jit(solution)/shard_map/ppermute | solution.py:409
  10.8 7.3 %collective-permute-start.7 = (bf16[2,112,512]{2,1,0:T(8,128)(2,1)S(1)}, bf16[2,112,512]{2,1,0:T(8,128)(2,1)S(1)}, u32[]{:S(2)}, u32[]{:S(2)}) collective-permute-start(bf16[2,112,512]{2,1,0:T(8,128)(2,1)S(1)} %broadcast_select_fusion.11), channel_id=1, source_target_pairs={{0,12},{4,8},{12,0},{8,4},{66,78},{70,74},{78,66},{74,70},{1,13},{... | collective-permute-start | bytes 688136 | tf_op jit(solution)/shard_map/ppermute | solution.py:409
  12.4 7.9 %collective-permute-start.1 = (bf16[2,112,512]{2,1,0:T(8,128)(2,1)S(1)}, bf16[2,112,512]{2,1,0:T(8,128)(2,1)S(1)}, u32[]{:S(2)}, u32[]{:S(2)}) collective-permute-start(bf16[2,112,512]{2,1,0:T(8,128)(2,1)S(1)} %broadcast_select_fusion.13), channel_id=1, source_target_pairs={{0,48},{16,32},{48,0},{32,16},{2,50},{18,34},{50,2},{34,18},{1,49}... | collective-permute-start | bytes 688136 | tf_op jit(solution)/shard_map/ppermute | solution.py:409
  15.5 6.5 %collective-permute-start.4 = (bf16[2,112,512]{2,1,0:T(8,128)(2,1)S(1)}, bf16[2,112,512]{2,1,0:T(8,128)(2,1)S(1)}, u32[]{:S(2)}, u32[]{:S(2)}) collective-permute-start(bf16[2,112,512]{2,1,0:T(8,128)(2,1)S(1)} %broadcast_select_fusion.12), channel_id=1, source_target_pairs={{0,16},{16,0},{48,32},{32,48},{2,18},{18,2},{50,34},{34,50},{1,17}... | collective-permute-start | bytes 688136 | tf_op jit(solution)/shard_map/ppermute | solution.py:409
  15.9 11.0 %collective-permute-start.11 = (bf16[2,2,112,512]{3,2,0,1:T(8,128)(2,1)S(1)}, bf16[2,2,112,512]{3,2,0,1:T(8,128)(2,1)S(1)}, u32[]{:S(2)}, u32[]{:S(2)}) collective-permute-start(bf16[2,2,112,512]{3,2,0,1:T(8,128)(2,1)S(1)} %broadcast_select_fusion.4), channel_id=1, source_target_pairs={{0,12},{4,8},{12,0},{8,4},{66,78},{70,74},{78,66},{74,70},{1,13},{... | collective-permute-start | bytes 1376264 | tf_op jit(solution)/shard_map/ppermute | solution.py:409
  18.2 11.5 %collective-permute-start.8 = (bf16[2,2,112,512]{3,2,1,0:T(8,128)(2,1)S(1)}, bf16[2,2,112,512]{3,2,1,0:T(8,128)(2,1)S(1)}, u32[]{:S(2)}, u32[]{:S(2)}) collective-permute-start(bf16[2,2,112,512]{3,2,1,0:T(8,128)(2,1)S(1)} %broadcast_select_fusion.6), channel_id=1, source_target_pairs={{0,66},{4,70},{12,78},{8,74},{66,0},{70,4},{78,12},{74,8},{1,67},{... | collective-permute-start | bytes 1376264 | tf_op jit(solution)/shard_map/ppermute | solution.py:409
  20.5 12.4 %collective-permute-start.2 = (bf16[2,2,112,512]{3,2,1,0:T(8,128)(2,1)S(1)}, bf16[2,2,112,512]{3,2,1,0:T(8,128)(2,1)S(1)}, u32[]{:S(2)}, u32[]{:S(2)}) collective-permute-start(bf16[2,2,112,512]{3,2,1,0:T(8,128)(2,1)S(1)} %broadcast_select_fusion.9), channel_id=1, source_target_pairs={{0,2},{16,18},{48,50},{32,34},{2,0},{18,16},{50,48},{34,32},{1,3},... | collective-permute-start | bytes 1376264 | tf_op jit(solution)/shard_map/ppermute | solution.py:409
  22.1 10.6 %collective-permute-start.5 = (bf16[2,2,112,512]{3,2,0,1:T(8,128)(2,1)S(1)}, bf16[2,2,112,512]{3,2,0,1:T(8,128)(2,1)S(1)}, u32[]{:S(2)}, u32[]{:S(2)}) collective-permute-start(bf16[2,2,112,512]{3,2,0,1:T(8,128)(2,1)S(1)} %broadcast_select_fusion.7), channel_id=1, source_target_pairs={{0,48},{16,32},{48,0},{32,16},{2,50},{18,34},{50,2},{34,18},{1,49}... | collective-permute-start | bytes 1376264 | tf_op jit(solution)/shard_map/ppermute | solution.py:409
  33.2 3.9 %collective-permute-start.12 = (bf16[1792,512]{1,0:T(8,128)(2,1)S(1)}, bf16[1792,512]{1,0:T(8,128)(2,1)S(1)}, u32[]{:S(2)}, u32[]{:S(2)}) collective-permute-start(bf16[1792,512]{1,0:T(8,128)(2,1)S(1)} %bitcast.40), channel_id=1, source_target_pairs={{0,1},{1,0},{2,3},{3,2},{4,5},{5,4},{6,7},{7,6},{8,9},{9,8},{10,11... | collective-permute-start | bytes 5505032 | tf_op jit(solution)/shard_map/ppermute | solution.py:413
  57.1 5.1 %collective-permute-start.13 = (f32[1,16,128]{2,1,0:T(8,128)}, f32[1,16,128]{2,1,0:T(8,128)S(1)}, u32[]{:S(2)}, u32[]{:S(2)}) collective-permute-start(f32[1,16,128]{2,1,0:T(8,128)} %get-tuple-element.29), channel_id=1, source_target_pairs={{0,66},{4,70},{12,78},{8,74},{66,0},{70,4},{78,12},{74,8},{1,67},{... | collective-permute-start | bytes 24584 | tf_op jit(solution)/shard_map/ppermute | solution.py:409
  62.9 6.5 %collective-permute-start.14 = (f32[1,16,128]{2,1,0:T(8,128)S(1)}, f32[1,16,128]{2,1,0:T(8,128)S(1)}, u32[]{:S(2)}, u32[]{:S(2)}) collective-permute-start(f32[1,16,128]{2,1,0:T(8,128)S(1)} %add_select_fusion.2), channel_id=1, source_target_pairs={{0,12},{4,8},{12,0},{8,4},{66,78},{70,74},{78,66},{74,70},{1,13},{... | collective-permute-start | bytes 24584 | tf_op jit(solution)/shard_map/ppermute | solution.py:409
  66.0 10.2 %all-to-all-start = ((f32[8,28,128]{2,1,0:T(8,128)}), f32[8,28,128]{2,1,0:T(8,128)S(1)}, u32[]{:S(2)}, u32[]{:S(2)}) async-start(f32[8,28,128]{2,1,0:T(8,128)} %broadcast_in_dim.307), calls=%async_computation | async-start | bytes 262144 | tf_op jit(solution)/shard_map/all_to_all | solution.py:417
  69.5 7.1 %collective-permute-start.15 = (f32[1,16,128]{2,1,0:T(8,128)S(1)}, f32[1,16,128]{2,1,0:T(8,128)S(1)}, u32[]{:S(2)}, u32[]{:S(2)}) collective-permute-start(f32[1,16,128]{2,1,0:T(8,128)S(1)} %add_select_fusion.1), channel_id=1, source_target_pairs={{0,4},{4,0},{12,8},{8,12},{66,70},{70,66},{78,74},{74,78},{1,5},{5... | collective-permute-start | bytes 24584 | tf_op jit(solution)/shard_map/ppermute | solution.py:409
  98.0 34.0 %all-to-all-start.2 = ((bf16[8,240,512]{2,1,0:T(8,128)(2,1)}), bf16[8,240,512]{2,1,0:T(8,128)(2,1)S(1)}, u32[]{:S(2)}, u32[]{:S(2)}) async-start(bf16[8,240,512]{2,1,0:T(8,128)(2,1)} %bitcast.44), calls=%async_computation.2 | async-start | bytes 3932160 | tf_op jit(solution)/shard_map/all_to_all | solution.py:417
  122.9 2.5 %collective-permute-start.18 = (bf16[448,512]{1,0:T(8,128)(2,1)}, bf16[448,512]{1,0:T(8,128)(2,1)S(1)}, u32[]{:S(2)}, u32[]{:S(2)}) collective-permute-start(bf16[448,512]{1,0:T(8,128)(2,1)} %get-tuple-element.39), channel_id=1, source_target_pairs={{0,1},{1,0},{2,3},{3,2},{4,5},{5,4},{6,7},{7,6},{8,9},{9,8},{10,11... | collective-permute-start | bytes 1376264 | tf_op jit(solution)/shard_map/ppermute | solution.py:413
  122.9 2.7 %collective-permute-start.19 = (bf16[448,512]{1,0:T(8,128)(2,1)}, bf16[448,512]{1,0:T(8,128)(2,1)S(1)}, u32[]{:S(2)}, u32[]{:S(2)}) collective-permute-start(bf16[448,512]{1,0:T(8,128)(2,1)} %get-tuple-element.40), channel_id=1, source_target_pairs={{0,1},{1,0},{2,3},{3,2},{4,5},{5,4},{6,7},{7,6},{8,9},{9,8},{10,11... | collective-permute-start | bytes 1376264 | tf_op jit(solution)/shard_map/ppermute | solution.py:413
  123.4 2.8 %collective-permute-start.20 = (bf16[448,512]{1,0:T(8,128)(2,1)}, bf16[448,512]{1,0:T(8,128)(2,1)S(1)}, u32[]{:S(2)}, u32[]{:S(2)}) collective-permute-start(bf16[448,512]{1,0:T(8,128)(2,1)} %get-tuple-element.41), channel_id=1, source_target_pairs={{0,1},{1,0},{2,3},{3,2},{4,5},{5,4},{6,7},{7,6},{8,9},{9,8},{10,11... | collective-permute-start | bytes 1376264 | tf_op jit(solution)/shard_map/ppermute | solution.py:413
  123.5 3.4 %collective-permute-start.21 = (bf16[448,512]{1,0:T(8,128)(2,1)}, bf16[448,512]{1,0:T(8,128)(2,1)S(1)}, u32[]{:S(2)}, u32[]{:S(2)}) collective-permute-start(bf16[448,512]{1,0:T(8,128)(2,1)} %get-tuple-element.42), channel_id=1, source_target_pairs={{0,1},{1,0},{2,3},{3,2},{4,5},{5,4},{6,7},{7,6},{8,9},{9,8},{10,11... | collective-permute-start | bytes 1376264 | tf_op jit(solution)/shard_map/ppermute | solution.py:413
  123.9 1.5 collective-permute-start.17
  133.4 31.5 %all-to-all-start.1 = ((bf16[8,240,512]{2,1,0:T(8,128)(2,1)}), bf16[8,240,512]{2,1,0:T(8,128)(2,1)}, u32[]{:S(2)}, u32[]{:S(2)}) async-start(bf16[8,240,512]{2,1,0:T(8,128)(2,1)} %bitcast.45), calls=%async_computation.1 | async-start | bytes 3932160 | tf_op jit(solution)/shard_map/all_to_all | solution.py:417
  (10 other events, 33.5 us)
